TPU v7x, 256 devices: a whole 4x4x8 slice. The times are simulated.
256 devices in a mesh: group: 32 (over y, z), seq: 8 (over x, core).
Axes of the slice: x: 4, y: 4, z: 8, core: 2. Of those that a mesh axis runs over, the one named last changes fastest.
Arguments:
- embed_table: bfloat16 [8192, 1024], P('group'), may hold values from -6 to 6
- adam_m: float32 [8192, 1024], P('group'), may hold values from -0.6 to 0.6
- adam_v: float32 [8192, 1024], P('group'), may hold values from 0.003 to 0.03
- lengths: int32 [32, 4], P('group'), may hold values from 1 to 1024, 2048 in all within a row
- row_owner: int32 [65536, 1], P(('group', 'seq')), may hold values from 0 to 31; in each aligned block of 256 rows (0 to 255, 256 to 511, ...) at most 16 rows name the same one
- row_index: int32 [65536], P(('group', 'seq')), may hold values from 0 to 255
- proj_weight: bfloat16 [1024, 4096], P(None, 'seq'), may hold values from -0.1875 to 0.1875
- out_weight: bfloat16 [1024, 1024], replicated, may hold values from -0.1875 to 0.1875
- norm_gain: float32 [1024], replicated, may hold values from 0.1 to 1.9
- upstream: bfloat16 [65536, 1024], P(('group', 'seq')), may hold values from -6 to 6
Outputs:
- layer_out: float32 [65536, 1024], P(('group', 'seq'))
- new_table: float32 [8192, 1024], P('group')
- new_moment: float32 [8192, 1024], P('group')
- new_second: float32 [8192, 1024], P('group')
Inputs may be any that keep to these rules, and one draw needn't show every extreme that they name: `row_owner`: among the 256 tokens of one device (aligned blocks), no owner is named more than 16 times, a bound that some block reaches. Each group's lengths sum to 2048; the longest is exactly 2048 // 2.
All inputs are finite; a program needn't handle non-finite values.
Results may differ from a plain program's by a relative error of at most 0.0053.
Values may be sent and summed in bfloat16 or wider, within the bound.
A program may use at most 128 MiB of HBM per device.

v0:
```python
import jax
import jax.numpy as jnp
from jax import lax
from jax.sharding import PartitionSpec as P

DH = 64


learn_rate = 0.05
beta_first = 0.9
beta_second = 0.999
adam_eps = 1e-08
norm_eps = 1e-05
bias_first = 1.0 - 0.9**10
bias_second = 1.0 - 0.999**10


def silu_pair(scores):
    sigma = jax.nn.sigmoid(scores)
    return (scores * sigma, sigma * (1.0 + scores * (1.0 - sigma)))


def norm_rows(attended, gain):
    center_val = jnp.mean(attended, axis=-1, keepdims=True)
    centered = attended - center_val
    spread = jnp.mean(centered * centered, axis=-1, keepdims=True)
    return centered * lax.rsqrt(spread + norm_eps) * gain


def finish(embedded, attended, units, norm_gain, out_weight, upstream):
    normed, pullback = jax.vjp(
        lambda inner: norm_rows(inner, norm_gain), attended.astype(jnp.float32)
    )
    unit_vals = units.astype(jnp.float32)
    mixed = (normed * unit_vals).astype(jnp.bfloat16)
    layer_out = embedded.astype(jnp.float32) + jnp.dot(
        mixed, out_weight, preferred_element_type=jnp.float32
    )
    d_mixed = jnp.dot(upstream, out_weight.T, preferred_element_type=jnp.float32)
    d_units = (d_mixed * normed).astype(jnp.bfloat16)
    d_attended = pullback(d_mixed * unit_vals)[0].astype(jnp.bfloat16)
    return (layer_out, d_units, d_attended)


def history_ids(group_lengths, group_tok):
    ends = jnp.cumsum(group_lengths)
    places = jnp.arange(group_tok, dtype=jnp.int32)
    return jnp.sum((places[:, None] >= ends[None, :]).astype(jnp.int32), axis=1)


def visible_block(history, places, offset, block_rows):
    query_history = lax.dynamic_slice_in_dim(history, offset, block_rows, 0)
    query_places = offset + jnp.arange(block_rows, dtype=jnp.int32)
    return (query_history[:, None] == history[None, :]) & (places[None, :] <= query_places[:, None])


def attend(parts, history, places, block_rows, score_scale):
    group_tok = parts.shape[0]
    query_all = parts[:, :, 0]
    key_part = parts[:, :, 1]
    value_part = parts[:, :, 2]

    def one_block(offset):
        query_part = lax.dynamic_slice_in_dim(query_all, offset, block_rows, 0)
        scores = score_scale * jnp.einsum(
            "qhd,khd->hqk", query_part, key_part, preferred_element_type=jnp.float32
        )
        visible = visible_block(history, places, offset, block_rows)
        weights = jnp.where(visible[None], silu_pair(scores)[0], 0.0).astype(jnp.bfloat16)
        return jnp.einsum(
            "hqk,khd->qhd", weights, value_part, preferred_element_type=jnp.float32
        ).astype(jnp.bfloat16)

    offsets = jnp.arange(group_tok // block_rows, dtype=jnp.int32) * block_rows
    blocks = lax.map(one_block, offsets)
    return blocks.reshape(group_tok, -1)


def attend_back(parts, d_heads, history, places, block_rows, score_scale):
    group_tok = parts.shape[0]
    query_all = parts[:, :, 0]
    key_part = parts[:, :, 1]
    value_part = parts[:, :, 2]

    def one_block(totals, offset):
        d_keys, d_values = totals
        query_part = lax.dynamic_slice_in_dim(query_all, offset, block_rows, 0)
        d_out = lax.dynamic_slice_in_dim(d_heads, offset, block_rows, 0)
        scores = score_scale * jnp.einsum(
            "qhd,khd->hqk", query_part, key_part, preferred_element_type=jnp.float32
        )
        activated, slope = silu_pair(scores)
        visible = visible_block(history, places, offset, block_rows)
        weights = jnp.where(visible[None], activated, 0.0).astype(jnp.bfloat16)
        d_weights = jnp.einsum(
            "qhd,khd->hqk", d_out, value_part, preferred_element_type=jnp.float32
        )
        d_scores = jnp.where(visible[None], d_weights * slope, 0.0).astype(jnp.bfloat16)
        d_query = (
            score_scale
            * jnp.einsum("hqk,khd->qhd", d_scores, key_part, preferred_element_type=jnp.float32)
        ).astype(jnp.bfloat16)
        d_keys = d_keys + score_scale * jnp.einsum(
            "hqk,qhd->khd", d_scores, query_part, preferred_element_type=jnp.float32
        )
        d_values = d_values + jnp.einsum(
            "hqk,qhd->khd", weights, d_out, preferred_element_type=jnp.float32
        )
        return ((d_keys, d_values), d_query)

    start_totals = (
        jnp.zeros(key_part.shape, jnp.float32),
        jnp.zeros(value_part.shape, jnp.float32),
    )
    offsets = jnp.arange(group_tok // block_rows, dtype=jnp.int32) * block_rows
    totals, d_queries = lax.scan(one_block, start_totals, offsets)
    d_queries = d_queries.reshape(key_part.shape)
    return jnp.stack(
        (d_queries, totals[0].astype(jnp.bfloat16), totals[1].astype(jnp.bfloat16)), axis=2
    )


def adam_update(embed_table, adam_m, adam_v, row_grad):
    new_moment = beta_first * adam_m + (1.0 - beta_first) * row_grad
    new_second = beta_second * adam_v + (1.0 - beta_second) * row_grad * row_grad
    step_size = new_moment / bias_first / (jnp.sqrt(new_second / bias_second) + adam_eps)
    new_table = embed_table.astype(jnp.float32) - learn_rate * step_size
    return (new_table, new_moment, new_second)


def body(
    embed_table,
    adam_m,
    adam_v,
    lengths,
    row_owner,
    row_index,
    proj_weight,
    out_weight,
    norm_gain,
    upstream,
):
    tok_rows = row_index.shape[0]
    group_count = lax.axis_size("group")
    shard_count = lax.axis_size("seq")
    capacity = 2 * tok_rows // group_count
    group_tok = tok_rows * shard_count
    head_count = proj_weight.shape[1] // (4 * DH)
    width = embed_table.shape[1]
    score_scale = DH ** (-0.5)
    block_rows = min(512, group_tok)
    destination = row_owner[:, 0]
    hits = (destination[:, None] == jnp.arange(group_count, dtype=jnp.int32)[None, :]).astype(
        jnp.int32
    )
    slot_index = jnp.sum((jnp.cumsum(hits, axis=0) - hits) * hits, axis=1)
    requests = (
        jnp.full((group_count, capacity), -1, jnp.int32).at[destination, slot_index].set(row_index)
    )
    asked = lax.all_to_all(requests, "group", split_axis=0, concat_axis=0, tiled=True)
    found = jnp.take(embed_table, jnp.maximum(asked, 0), axis=0)
    found = jnp.where((asked >= 0)[:, :, None], found, jnp.zeros_like(found))
    returned = lax.all_to_all(found, "group", split_axis=0, concat_axis=0, tiled=True)
    embedded = returned[destination, slot_index]
    history = history_ids(lengths[0], group_tok)
    places = jnp.arange(group_tok, dtype=jnp.int32)
    full_weight = lax.all_gather(proj_weight, "seq", axis=1, tiled=True)
    pre_tokens = jnp.dot(embedded, full_weight, preferred_element_type=jnp.float32)
    activated, slope_pre = silu_pair(pre_tokens)
    proj_tokens = activated.astype(jnp.bfloat16)
    proj_heads = lax.all_to_all(proj_tokens, "seq", split_axis=1, concat_axis=0, tiled=True)
    parts = proj_heads.reshape(group_tok, head_count, 4, DH)
    attended_heads = attend(parts, history, places, block_rows, score_scale)
    attended = lax.all_to_all(attended_heads, "seq", split_axis=0, concat_axis=1, tiled=True)
    units = proj_tokens.reshape(tok_rows, -1, 4, DH)[:, :, 3].reshape(tok_rows, -1)
    layer_out, d_units, d_attended = finish(
        embedded, attended, units, norm_gain, out_weight, upstream
    )
    d_heads = lax.all_to_all(d_attended, "seq", split_axis=1, concat_axis=0, tiled=True)
    d_qkv = attend_back(
        parts, d_heads.reshape(group_tok, head_count, DH), history, places, block_rows, score_scale
    )
    qkv_tokens = lax.all_to_all(
        d_qkv.reshape(group_tok, head_count * 3 * DH),
        "seq",
        split_axis=0,
        concat_axis=1,
        tiled=True,
    )
    d_proj = jnp.concatenate(
        (qkv_tokens.reshape(tok_rows, -1, 3, DH), d_units.reshape(tok_rows, -1, 1, DH)), axis=2
    )
    d_proj = d_proj.reshape(tok_rows, -1)
    d_pre = (d_proj.astype(jnp.float32) * slope_pre).astype(jnp.bfloat16)
    d_embedded = upstream.astype(jnp.float32) + jnp.dot(
        d_pre, full_weight.T, preferred_element_type=jnp.float32
    )
    outgoing = (
        jnp.zeros((group_count, capacity, width), jnp.float32)
        .at[destination, slot_index]
        .set(d_embedded)
    )
    incoming = lax.all_to_all(outgoing, "group", split_axis=0, concat_axis=0, tiled=True)
    table_rows = embed_table.shape[0]
    matches = (
        jnp.arange(table_rows, dtype=jnp.int32)[:, None] == asked.reshape(-1)[None, :]
    ).astype(jnp.float32)
    partial_grad = jnp.dot(matches, incoming.reshape(-1, width), precision=lax.Precision.HIGHEST)
    row_grad = lax.psum(partial_grad, "seq")
    new_table, new_moment, new_second = adam_update(embed_table, adam_m, adam_v, row_grad)
    return (layer_out, new_table, new_moment, new_second)


def solution(mesh):
    placed = (
        P("group", None),
        P("group", None),
        P("group", None),
        P("group", None),
        P(("group", "seq"), None),
        P(("group", "seq")),
        P(None, "seq"),
        P(),
        P(),
        P(("group", "seq"), None),
    )
    return jax.shard_map(
        body,
        mesh=mesh,
        in_specs=placed,
        out_specs=(P(("group", "seq"), None), P("group", None), P("group", None), P("group", None)),
        check_vma=False,
    )
```

profile of v0, /device:TPU:1, one launch (start us, length us, event | category | flops | bytes accessed | tf_op | source)
XLA Modules:
  0.0 546.3 jit_solution(16249571938387242233)
XLA Ops:
  10.9 21.7 %scatter_fusion = s32[32,16]{0,1:T(8,128)S(1)} fusion(s32[32,16]{0,1:T(8,128)S(1)} %broadcast_in_dim.89, s32[256]{0:T(256)S(1)} %bitcast.148, s32[256]{0:T(256)} %param.19), kind=kCustom, calls=%fused_computation.2 | custom fusion | bytes 5120 | tf_op jit(solution)/shard_map/scatter | solution.py:158
  32.7 20.5 %all_to_all.80 = s32[32,1,16]{2,1,0:T(1,128)S(1)} all-to-all(s32[32,1,16]{2,1,0:T(1,128)S(1)} %copy.78), channel_id=1, replica_groups=mesh['group'=32,'seq'=8] {'group'}, dimensions={0} | all-to-all | bytes 4096 | tf_op jit(solution)/shard_map/all_to_all | solution.py:160
  53.6 2.8 gather_fusion
  57.9 27.4 %all_to_all.81 = bf16[32,16,1024]{2,1,0:T(8,128)(2,1)S(1)} all-to-all(bf16[32,16,1024]{2,1,0:T(8,128)(2,1)S(1)} %select_select_fusion), channel_id=1, replica_groups=mesh['group'=32,'seq'=8] {'group'}, dimensions={0} | all-to-all | bytes 2097152 | tf_op jit(solution)/shard_map/all_to_all | solution.py:163
  85.3 3.6 gather_fusion.1
  88.9 8.5 %multiply_convert_fusion.1 = (bf16[256,4096]{1,0:T(8,128)(2,1)}, f32[256,4096]{1,0:T(8,128)}) fusion(bf16[256,1024]{1,0:T(8,128)(2,1)} %gather_fusion.1, bf16[1024,4096]{1,0:T(8,128)(2,1)} %all-gather.2.cloned.1.call-done), kind=kOutput, calls=%fused_computation.48 | convolution fusion | flops 2152726528 | bytes 15204352 | tf_op jit(solution)/shard_map/dot_general | solution.py:168
  97.4 4.1 copy.100
  101.5 10.1 %all-to-all-start.2 = ((bf16[256,8,512]{0,2,1:T(8,128)(2,1)}), bf16[256,8,512]{0,2,1:T(8,128)(2,1)}, u32[]{:S(2)}, u32[]{:S(2)}) async-start(bf16[256,8,512]{0,2,1:T(8,128)(2,1)} %bitcast.151), calls=%async_computation.2 | async-start | bytes 4194304 | tf_op jit(solution)/shard_map/all_to_all | solution.py:171
  111.8 26.1 %all-to-all-done.2 = bf16[256,8,512]{0,2,1:T(8,128)(2,1)} async-done(((bf16[256,8,512]{0,2,1:T(8,128)(2,1)}), bf16[256,8,512]{0,2,1:T(8,128)(2,1)}, u32[]{:S(2)}, u32[]{:S(2)}) %all-to-all-start.2) | async-done | bytes 2097184 | tf_op jit(solution)/shard_map/all_to_all | solution.py:171
  137.9 4.1 copy.85
  142.0 4.2 reshape.291
  149.3 46.2 %while.26 = (s32[]{:T(128)}, bf16[4,512,2,64]{1,3,2,0:T(8,128)(2,1)}, s32[4]{0:T(128)S(1)}, s32[2048]{0:T(1024)S(1)}, bf16[2048,2,64]{0,2,1:T(8,128)(2,1)S(1)}, ...) while((s32[]{:T(128)}, ...), condition=%wide.region_7.8_spmd.clone, body=%wide.region_6.7_spmd.clone.sunk | while | flops 554762752 | bytes 3426475 | solution.py:75
  154.8 6.1 %fusion.94 = bf16[4,512,2,64]{1,3,2,0:T(8,128)(2,1)} fusion(bf16[4,512,2,64]{1,3,2,0:T(8,128)(2,1)} %get-tuple-element.340, s32[]{:T(128)S(6)} %copy.112, bf16[2048,2,64]{0,2,1:T(8,128)(2,1)} %get-tuple-element.355, bf16[2048,2,64]{0,2,1:T(8,128)(2,1)S(1)} %get-tuple-element.354, pred[512,2048]{1,0:T(8,128)(4,1)} %fusion.93, ...), kind=kOutput, calls=%fused_computation.12.clone.1 | convolution fusion | flops 551616512 | bytes 2359304 | tf_op jit(solution)/shard_map/while/body/eval_jaxpr/hqk,khd->qhd/dot_general | solution.py:70
  166.3 6.1 %fusion.94 = bf16[4,512,2,64]{1,3,2,0:T(8,128)(2,1)} fusion(bf16[4,512,2,64]{1,3,2,0:T(8,128)(2,1)} %get-tuple-element.340, s32[]{:T(128)S(6)} %copy.112, bf16[2048,2,64]{0,2,1:T(8,128)(2,1)} %get-tuple-element.355, bf16[2048,2,64]{0,2,1:T(8,128)(2,1)S(1)} %get-tuple-element.354, pred[512,2048]{1,0:T(8,128)(4,1)} %fusion.93, ...), kind=kOutput, calls=%fused_computation.12.clone.1 | convolution fusion | flops 551616512 | bytes 2359304 | tf_op jit(solution)/shard_map/while/body/eval_jaxpr/hqk,khd->qhd/dot_general | solution.py:70
  177.9 6.1 %fusion.94 = bf16[4,512,2,64]{1,3,2,0:T(8,128)(2,1)} fusion(bf16[4,512,2,64]{1,3,2,0:T(8,128)(2,1)} %get-tuple-element.340, s32[]{:T(128)S(6)} %copy.112, bf16[2048,2,64]{0,2,1:T(8,128)(2,1)} %get-tuple-element.355, bf16[2048,2,64]{0,2,1:T(8,128)(2,1)S(1)} %get-tuple-element.354, pred[512,2048]{1,0:T(8,128)(4,1)} %fusion.93, ...), kind=kOutput, calls=%fused_computation.12.clone.1 | convolution fusion | flops 551616512 | bytes 2359304 | tf_op jit(solution)/shard_map/while/body/eval_jaxpr/hqk,khd->qhd/dot_general | solution.py:70
  189.4 6.1 %fusion.94 = bf16[4,512,2,64]{1,3,2,0:T(8,128)(2,1)} fusion(bf16[4,512,2,64]{1,3,2,0:T(8,128)(2,1)} %get-tuple-element.340, s32[]{:T(128)S(6)} %copy.112, bf16[2048,2,64]{0,2,1:T(8,128)(2,1)} %get-tuple-element.355, bf16[2048,2,64]{0,2,1:T(8,128)(2,1)S(1)} %get-tuple-element.354, pred[512,2048]{1,0:T(8,128)(4,1)} %fusion.93, ...), kind=kOutput, calls=%fused_computation.12.clone.1 | convolution fusion | flops 551616512 | bytes 2359304 | tf_op jit(solution)/shard_map/while/body/eval_jaxpr/hqk,khd->qhd/dot_general | solution.py:70
  195.5 2.6 copy.86
  202.0 4.9 all-to-all-start.3
  209.1 2.5 copy.90
  211.6 4.9 all-to-all-done.3
  219.9 2.5 copy.101
  228.5 5.1 all-to-all-start.4
  233.6 9.5 %all-to-all-done.4 = bf16[256,8,128]{2,0,1:T(8,128)(2,1)} async-done(((bf16[256,8,128]{2,0,1:T(8,128)(2,1)}), bf16[256,8,128]{2,0,1:T(8,128)(2,1)}, u32[]{:S(2)}, u32[]{:S(2)}) %all-to-all-start.4) | async-done | bytes 524320 | tf_op jit(solution)/shard_map/all_to_all | solution.py:179
  248.4 74.5 %while.27 = (s32[]{:T(128)}, f32[2048,2,64]{0,2,1:T(8,128)S(1)}, f32[2048,2,64]{0,2,1:T(8,128)}, bf16[4,512,2,64]{1,3,2,0:T(8,128)(2,1)}, s32[4]{0:T(128)S(1)}, ...) while((s32[]{:T(128)}, f32[2048,2,64]{0,2,1:T(8,128)S(1)}, ...), condition=%wide.region_13.14_spmd.clone, body=%wide.region_12.13_spmd.clone.sunk | while | flops 1384514048 | bytes 62015844 | solution.py:116
  252.5 2.6 fusion.104
  255.2 3.2 fusion.107
  258.4 4.5 select_convert_fusion.11
  271.1 2.6 fusion.104
  273.8 3.2 fusion.107
  277.0 4.5 select_convert_fusion.11
  289.7 2.6 fusion.104
  292.3 3.2 fusion.107
  295.6 4.5 select_convert_fusion.11
  308.3 2.6 fusion.104
  310.9 3.2 fusion.107
  314.2 4.5 select_convert_fusion.11
  332.1 5.1 all-to-all-start.5
  337.4 20.6 %all-to-all-done.5 = bf16[8,256,384]{1,2,0:T(8,128)(2,1)} async-done(((bf16[8,256,384]{1,2,0:T(8,128)(2,1)}), bf16[8,256,384]{1,2,0:T(8,128)(2,1)}, u32[]{:S(2)}, u32[]{:S(2)}) %all-to-all-start.5) | async-done | bytes 1572896 | tf_op jit(solution)/shard_map/all_to_all | solution.py:183
  359.6 2.4 bitcast_convert_fusion
  362.0 5.6 %copy.99 = f32[256,4096]{1,0:T(8,128)} copy(f32[256,4096]{0,1:T(8,128)} %bitcast_convert_fusion) | data formatting | bytes 8388608 | tf_op jit(solution)/shard_map/convert_element_type | solution.py:194
  367.7 8.8 %fusion.38 = f32[256,1024]{1,0:T(8,128)S(1)} fusion(bf16[1024,4096]{1,0:T(8,128)(2,1)} %all-gather.2.cloned.1.call-done, f32[256,4096]{1,0:T(8,128)} %copy.99, f32[256,4096]{1,0:T(8,128)} %get-tuple-element.220, bf16[256,1024]{1,0:T(8,128)(2,1)} %param.23), kind=kOutput, calls=%fused_computation.57 | convolution fusion | flops 2157445120 | bytes 18350080 | tf_op jit(solution)/shard_map/dot_general | solution.py:195
  378.1 36.3 %scatter_fusion.1 = f32[32,16,1024]{2,1,0:T(8,128)} fusion(f32[32,16,1024]{2,1,0:T(8,128)} %broadcast_in_dim.94, s32[256]{0:T(256)S(1)} %bitcast.149, f32[256,1024]{1,0:T(8,128)S(1)} %fusion.38), kind=kCustom, calls=%fused_computation.3 | custom fusion | bytes 3147776 | tf_op jit(solution)/shard_map/scatter | solution.py:201
  414.4 4.9 all-to-all-start.6
  420.7 47.3 %all-to-all-done.6 = f32[32,16,1024]{2,1,0:T(8,128)} async-done(((f32[32,16,1024]{2,1,0:T(8,128)}), f32[32,16,1024]{2,1,0:T(8,128)}, u32[]{:S(2)}, u32[]{:S(2)}) %all-to-all-start.6) | async-done | bytes 2097184 | tf_op jit(solution)/shard_map/all_to_all | solution.py:203
  468.0 3.8 fusion.44
  471.9 3.3 convolution_add_fusion
  475.2 59.8 %all-reduce.2.cloned.1.call-done = f32[256,1024]{1,0:T(8,128)} async-done(((f32[256,1024]{1,0:T(8,128)}), f32[256,1024]{1,0:T(8,128)}) %all-reduce.2.cloned.1.call-update) | async-done | bytes 1048592 | tf_op jit(solution)/shard_map/psum | solution.py:209
  535.1 4.1 multiply_subtract_fusion
  (179 shorter events, 83.4 us)
Async XLA Ops:
  7.2 215.3 %copy-start = (bf16[1024,1024]{1,0:T(8,128)(2,1)S(1)}, bf16[1024,1024]{1,0:T(8,128)(2,1)}, u32[]{:S(2)}) copy-start(bf16[1024,1024]{1,0:T(8,128)(2,1)} %param.21) | copy-start | bytes 6291460
  7.2 46.5 %copy-start.1 = (bf16[256,1024]{1,0:T(8,128)(2,1)S(1)}, bf16[256,1024]{1,0:T(8,128)(2,1)}, u32[]{:S(2)}) copy-start(bf16[256,1024]{1,0:T(8,128)(2,1)} %param.14) | copy-start | bytes 1572868
  7.2 81.7 %all-gather.2.cloned.1.call-start = ((), (), s32[]{:S(2)}) async-start(), calls=%async_computation.7 | async-start | bytes 9437184 | tf_op jit(solution)/shard_map/all_gather | solution.py:167
  10.9 45.5 %copy-start.3 = (s32[256,1]{0,1:T(1,128)}, s32[256,1]{0,1:T(1,128)S(1)}, u32[]{:S(2)}) copy-start(s32[256,1]{0,1:T(1,128)S(1)} %get-tuple-element.209) | copy-start | bytes 3076
  53.2 3.2 copy-start.16
  97.4 14.2 %copy-start.24 = (s32[1,4]{1,0:T(1,128)S(1)}, s32[1,4]{1,0:T(1,128)}, u32[]{:S(2)}) copy-start(s32[1,4]{1,0:T(1,128)} %param.17) | copy-start | bytes 52
  101.5 36.5 %all-to-all-start.2 = ((bf16[256,8,512]{0,2,1:T(8,128)(2,1)}), bf16[256,8,512]{0,2,1:T(8,128)(2,1)}, u32[]{:S(2)}, u32[]{:S(2)}) async-start(bf16[256,8,512]{0,2,1:T(8,128)(2,1)} %bitcast.151), calls=%async_computation.2 | async-start | bytes 4194304 | tf_op jit(solution)/shard_map/all_to_all | solution.py:171
  195.5 16.1 %copy-start.5 = (bf16[2048,2,64]{0,2,1:T(8,128)(2,1)}, bf16[2048,2,64]{0,2,1:T(8,128)(2,1)S(1)}, u32[]{:S(2)}) copy-start(bf16[2048,2,64]{0,2,1:T(8,128)(2,1)S(1)} %get-tuple-element.402) | copy-start | bytes 1572868
  195.5 16.1 %copy-start.9 = (bf16[2048,2,64]{0,2,1:T(8,128)(2,1)}, bf16[2048,2,64]{0,2,1:T(8,128)(2,1)S(1)}, u32[]{:S(2)}) copy-start(bf16[2048,2,64]{0,2,1:T(8,128)(2,1)S(1)} %get-tuple-element.405) | copy-start | bytes 1572868
  202.0 14.5 %all-to-all-start.3 = ((bf16[8,256,128]{1,2,0:T(8,128)(2,1)}), bf16[8,256,128]{1,2,0:T(8,128)(2,1)}, u32[]{:S(2)}, u32[]{:S(2)}) async-start(bf16[8,256,128]{1,2,0:T(8,128)(2,1)} %copy.87), calls=%async_computation.3 | async-start | bytes 1048576 | tf_op jit(solution)/shard_map/all_to_all | solution.py:174
  208.0 14.5 %copy-start.18 = (f32[1024]{0:T(1024)S(1)}, f32[1024]{0:T(1024)}, u32[]{:S(2)}) copy-start(f32[1024]{0:T(1024)} %param.22) | copy-start | bytes 12292
  216.5 5.9 %copy-start.7 = (f32[256,1024]{1,0:T(8,128)S(1)}, f32[256,1024]{1,0:T(8,128)}, u32[]{:S(2)}) copy-start(f32[256,1024]{1,0:T(8,128)} %copy.90) | copy-start | bytes 3145732
  217.8 8.3 %copy-start.20 = (f32[256]{0:T(256)}, f32[256]{0:T(256)S(1)}, u32[]{:S(2)}) copy-start(f32[256]{0:T(256)S(1)} %broadcast_multiply_fusion) | copy-start | bytes 3076
  222.4 3.7 copy-start.8
  226.1 1.4 copy-start.22
  228.5 14.7 %all-to-all-start.4 = ((bf16[256,8,128]{2,0,1:T(8,128)(2,1)}), bf16[256,8,128]{2,0,1:T(8,128)(2,1)}, u32[]{:S(2)}, u32[]{:S(2)}) async-start(bf16[256,8,128]{2,0,1:T(8,128)(2,1)} %copy_bitcast_fusion), calls=%async_computation.4 | async-start | bytes 1048576 | tf_op jit(solution)/shard_map/all_to_all | solution.py:179
  252.5 2.7 copy-start.12
  252.5 2.7 copy-start.14
  255.2 3.2 copy-start.15
  258.4 4.5 copy-start.13
  258.4 4.5 copy-start.6
  271.1 2.7 copy-start.12
  271.1 2.7 copy-start.14
  273.7 3.2 copy-start.15
  277.0 4.5 copy-start.13
  277.0 4.5 copy-start.6
  289.7 2.7 copy-start.12
  289.7 2.7 copy-start.14
  292.3 3.2 copy-start.15
  295.6 4.5 copy-start.13
  295.6 4.5 copy-start.6
  308.3 2.6 copy-start.12
  308.3 2.6 copy-start.14
  310.9 3.2 copy-start.15
  314.2 4.5 copy-start.13
  314.2 4.5 copy-start.6
  330.2 7.0 %copy-start.11 = (bf16[256,1024]{1,0:T(8,128)(2,1)S(1)}, bf16[256,1024]{1,0:T(8,128)(2,1)}, u32[]{:S(2)}) copy-start(bf16[256,1024]{1,0:T(8,128)(2,1)} %get-tuple-element.211) | copy-start | bytes 1572868
  332.1 25.9 %all-to-all-start.5 = ((bf16[8,256,384]{1,2,0:T(8,128)(2,1)}), bf16[8,256,384]{1,2,0:T(8,128)(2,1)}, u32[]{:S(2)}, u32[]{:S(2)}) async-start(bf16[8,256,384]{1,2,0:T(8,128)(2,1)} %copy.96), calls=%async_computation.5 | async-start | bytes 3145728 | tf_op jit(solution)/shard_map/all_to_all | solution.py:183
  367.7 10.4 %copy-start.4 = (s32[256,1]{0,1:T(1,128)S(1)}, s32[256,1]{0,1:T(1,128)}, u32[]{:S(2)}) copy-start(s32[256,1]{0,1:T(1,128)} %copy-done.3) | copy-start | bytes 3076
  414.4 5.5 %copy-start.17 = (s32[32,1,16]{2,1,0:T(1,128)S(1)}, s32[32,1,16]{2,1,0:T(1,128)}, u32[]{:S(2)}) copy-start(s32[32,1,16]{2,1,0:T(1,128)} %copy-done.16) | copy-start | bytes 6148
  414.4 57.4 %copy-start.10 = (bf16[256,1024]{1,0:T(8,128)(2,1)S(1)}, bf16[256,1024]{1,0:T(8,128)(2,1)}, u32[]{:S(2)}) copy-start(bf16[256,1024]{1,0:T(8,128)(2,1)} %gather_fusion.1) | copy-start | bytes 1572868
  414.4 57.5 %copy-start.19 = (f32[1024]{0:T(1024)S(1)}, f32[1024]{0:T(1024)}, u32[]{:S(2)}) copy-start(f32[1024]{0:T(1024)} %param.22) | copy-start | bytes 12292
  414.4 57.5 %copy-start.21 = (f32[256]{0:T(256)S(1)}, f32[256]{0:T(256)}, u32[]{:S(2)}) copy-start(f32[256]{0:T(256)} %copy-done.20) | copy-start | bytes 3076
  414.4 57.5 %copy-start.23 = (f32[256]{0:T(256)S(1)}, f32[256]{0:T(256)}, u32[]{:S(2)}) copy-start(f32[256]{0:T(256)} %copy-done.22) | copy-start | bytes 3076
  414.4 53.6 %all-to-all-start.6 = ((f32[32,16,1024]{2,1,0:T(8,128)}), f32[32,16,1024]{2,1,0:T(8,128)}, u32[]{:S(2)}, u32[]{:S(2)}) async-start(f32[32,16,1024]{2,1,0:T(8,128)} %scatter_fusion.1), calls=%async_computation.6 | async-start | bytes 4194304 | tf_op jit(solution)/shard_map/all_to_all | solution.py:203
  419.4 115.7 %all-reduce.2.cloned.1.call-start = ((), (), s32[]{:S(2)}) async-start(), calls=%async_computation.8 | async-start | bytes 2097152 | tf_op jit(solution)/shard_map/psum | solution.py:209
  471.8 63.2 %copy-start.2 = (bf16[256,1024]{1,0:T(8,128)(2,1)S(1)}, bf16[256,1024]{1,0:T(8,128)(2,1)}, u32[]{:S(2)}) copy-start(bf16[256,1024]{1,0:T(8,128)(2,1)} %param.14) | copy-start | bytes 1572868
Sparse Core Ops, SparseCore 0:
  9.9 56.4 all-gather.1
  472.0 63.0 all-reduce.1
where the time goes:
time: 557 us; the launch traced here: 546 us
  waiting for transfers between devices  169 us (30%)
  local copies, waits for them, and re-layouts  119 us (21%)
  matrix products  109 us (20%)
  blocking collectives  47.9 us (9%)
  other arithmetic  42.2 us (8%)
  starting transfers between devices  30.1 us (5%)
  loops' own time  15.3 us (3%)
  between operations  14.6 us (3%)
    psum x1, waiting for transfers between devices, body(): row_grad = lax.psum(partial_grad, 'seq')  59.8 us
    all_to_all x1, waiting for transfers between devices, body(): lax.all_to_all(outgoing, 'group', split_axis=0, concat_axis=0, tiled=True)  47.3 us
    scatter x1, local copies, waits for them, and re-layouts, body(): outgoing = jnp.zeros((group_count, capacity, width), jnp.float32).at[dest...  36.3 us
    all_to_all x1, blocking collectives, body(): lax.all_to_all(found, 'group', split_axis=0, concat_axis=0, tiled=True)  27.4 us
    all_to_all x1, waiting for transfers between devices, body(): lax.all_to_all(proj_tokens, 'seq', split_axis=1, concat_axis=0, tiled=True)  26.1 us
    dot_general x4, matrix products, one_block(): jnp.einsum('hqk,khd->qhd', weights, value_part, preferred_element_type=jn...  24.5 us
    scatter x1, local copies, waits for them, and re-layouts, body(): jnp.full((group_count, capacity), -1, jnp.int32).at[destination, slot_index]  21.7 us
    all_to_all x1, waiting for transfers between devices, body(): lax.all_to_all(d_qkv.reshape(group_tok, head_count * 3 * DH), 'seq', spli...  20.6 us
  transfers between devices with their start and end apart: 7, of which 6 were waited for; matrix products, arithmetic and copies ran while one was open for 8% of the time, Pallas kernels for 0%

commit v1 on v0

v1 whole, which is shorter than its diff:
```python
import functools

import jax
import jax.numpy as jnp
from jax import lax
from jax.experimental import pallas as pl
from jax.experimental.pallas import tpu as pltpu
from jax.sharding import PartitionSpec as P

DH = 64
PAIR = 2 * DH
SCALE = DH ** (-0.5)

learn_rate = 0.05
beta_first = 0.9
beta_second = 0.999
adam_eps = 1e-08
norm_eps = 1e-05
bias_first = 1.0 - 0.9**10
bias_second = 1.0 - 0.999**10

BF = jnp.bfloat16
F32 = jnp.float32
BLOCK = 256
NT = (((1,), (1,)), ((), ()))
TN = (((0,), (0,)), ((), ()))


def mm(a, b, dims=(((1,), (0,)), ((), ()))):
    return lax.dot_general(a, b, dims, preferred_element_type=F32)


def sigmoid(v):
    return 0.5 * jnp.tanh(0.5 * v) + 0.5


def silu_pair(v):
    sigma = sigmoid(v)
    act = v * sigma
    return act, sigma + act * (1.0 - sigma)


def ends_of(len_ref):
    e0 = len_ref[0, 0]
    e1 = e0 + len_ref[0, 1]
    e2 = e1 + len_ref[0, 2]
    return e0, e1, e2


def start_at(i, ends):
    e0, e1, e2 = ends
    return jnp.where(i >= e2, e2, jnp.where(i >= e1, e1, jnp.where(i >= e0, e0, 0)))


def stop_at(i, ends, total):
    e0, e1, e2 = ends
    return jnp.where(i >= e2, total, jnp.where(i >= e1, e2, jnp.where(i >= e0, e1, e0)))


def by_head(x):
    lane = lax.broadcasted_iota(jnp.int32, x.shape, 1)
    zero = jnp.zeros_like(x)
    return jnp.concatenate([jnp.where(lane < DH, x, zero), jnp.where(lane < DH, zero, x)], axis=0)


def merge_heads(x):
    half = x.shape[0] // 2
    lane = lax.broadcasted_iota(jnp.int32, (half, x.shape[1]), 1)
    return jnp.where(lane < DH, x[:half], x[half:])


def attend_kernel(len_ref, qkv_ref, out_ref):
    tokens = qkv_ref.shape[0]
    ends = ends_of(len_ref)

    @pl.loop(0, tokens // BLOCK)
    def _(qb):
        q0 = qb * BLOCK
        qs = by_head(qkv_ref[pl.ds(q0, BLOCK), 0:PAIR]) * jnp.asarray(SCALE, BF)
        row = lax.broadcasted_iota(jnp.int32, (2 * BLOCK, 1), 0)
        i = q0 + jnp.where(row >= BLOCK, row - BLOCK, row)
        start_i = start_at(i, ends)

        def step(kb, acc):
            k0 = kb * BLOCK
            k = qkv_ref[pl.ds(k0, BLOCK), PAIR : 2 * PAIR]
            v = qkv_ref[pl.ds(k0, BLOCK), 2 * PAIR : 3 * PAIR]
            s = mm(qs, k, NT)
            j = k0 + lax.broadcasted_iota(jnp.int32, s.shape, 1)
            visible = (j >= start_i) & (j <= i)
            w = jnp.where(visible, s * sigmoid(s), 0.0).astype(BF)
            return acc + mm(w, v)

        first = lax.div(start_at(q0, ends), BLOCK)
        acc = lax.fori_loop(first, qb + 1, step, jnp.zeros((2 * BLOCK, PAIR), F32))
        out_ref[pl.ds(q0, BLOCK), :] = merge_heads(acc).astype(BF)


def attend_back_kernel(len_ref, qkv_ref, pre_ref, do_ref, out_ref, dq_ref):
    tokens = qkv_ref.shape[0]
    ends = ends_of(len_ref)
    dq_ref[...] = jnp.zeros_like(dq_ref)

    def finish_part(rows, part, d_part):
        slope = silu_pair(pre_ref[rows, part * PAIR : (part + 1) * PAIR])[1]
        out_ref[rows, part * PAIR : (part + 1) * PAIR] = (d_part.astype(BF).astype(F32) * slope).astype(BF)

    @pl.loop(0, tokens // BLOCK)
    def _(kb):
        k0 = kb * BLOCK
        rows = pl.ds(k0, BLOCK)
        k = qkv_ref[rows, PAIR : 2 * PAIR]
        v = qkv_ref[rows, 2 * PAIR : 3 * PAIR]

        def step(qb, carry):
            dk, dv = carry
            q0 = qb * BLOCK
            qs = by_head(qkv_ref[pl.ds(q0, BLOCK), 0:PAIR]) * jnp.asarray(SCALE, BF)
            dos = by_head(do_ref[pl.ds(q0, BLOCK), :])
            s = mm(k, qs, NT)
            dw = mm(v, dos, NT)
            act, slope = silu_pair(s)
            col = lax.broadcasted_iota(jnp.int32, (1, 2 * BLOCK), 1)
            i = q0 + jnp.where(col >= BLOCK, col - BLOCK, col)
            start_i = start_at(i, ends)
            j = k0 + lax.broadcasted_iota(jnp.int32, s.shape, 0)
            visible = (j >= start_i) & (j <= i)
            w = jnp.where(visible, act, 0.0).astype(BF)
            ds = jnp.where(visible, dw * slope, 0.0).astype(BF)
            dq = mm(ds, k, TN)
            dq_ref[pl.ds(q0, BLOCK), :] += merge_heads(dq)
            return dk + mm(ds, qs), dv + mm(w, dos)

        last = lax.div(stop_at(k0 + BLOCK - 1, ends, tokens) - 1, BLOCK)
        zero = jnp.zeros((BLOCK, PAIR), F32)
        dk, dv = lax.fori_loop(kb, last + 1, step, (zero, zero))
        finish_part(rows, 0, dq_ref[rows, :] * SCALE)
        finish_part(rows, 1, dk)
        finish_part(rows, 2, dv)


def finish_kernel(att_ref, emb_ref, wu_ref, wo_ref, gain_ref, up_ref, layer_ref, datt_ref, dpu_ref):
    seq = wu_ref.shape[0]
    emb = emb_ref[...]
    d_mixed = mm(up_ref[...], wo_ref[...], NT)
    x = att_ref[...].astype(F32)
    center = x - jnp.mean(x, axis=-1, keepdims=True)
    spread = jnp.mean(center * center, axis=-1, keepdims=True)
    r = lax.rsqrt(spread + norm_eps)
    xhat = center * r
    gain = gain_ref[...]
    normed = xhat * gain
    pre_u = jnp.concatenate([mm(emb, wu_ref[s]) for s in range(seq)], axis=1)
    act_u, slope_u = silu_pair(pre_u)
    u = act_u.astype(BF).astype(F32)
    mixed = (normed * u).astype(BF)
    layer_ref[...] = emb.astype(F32) + mm(mixed, wo_ref[...])
    dpu_ref[...] = ((d_mixed * normed).astype(BF).astype(F32) * slope_u).astype(BF)
    gx = d_mixed * u * gain
    datt = r * (
        gx
        - jnp.mean(gx, axis=-1, keepdims=True)
        - xhat * jnp.mean(gx * xhat, axis=-1, keepdims=True)
    )
    datt_ref[...] = datt.astype(BF)


def d_embed_kernel(pos_ref, dqkv_ref, dpu_ref, w_ref, up_ref, out_ref):
    seq = w_ref.shape[0]
    d_emb = up_ref[...].astype(F32)
    for s in range(seq):
        d_emb = d_emb + mm(dqkv_ref[s], w_ref[s][:, : 3 * PAIR], NT)
        d_emb = d_emb + mm(dpu_ref[:, s * PAIR : (s + 1) * PAIR], w_ref[s][:, 3 * PAIR :], NT)
    slots = out_ref.shape[0]
    slot = lax.broadcasted_iota(jnp.int32, (slots, pos_ref.shape[1]), 0)
    place = jnp.where(slot == pos_ref[...], 1.0, 0.0).astype(BF)
    out_ref[...] = mm(place, d_emb.astype(BF)).astype(BF)


VM = pl.BlockSpec(memory_space=pltpu.VMEM)
SM = pl.BlockSpec(memory_space=pltpu.SMEM)
MIB = 1 << 20


def local_call(kernel, out_shape, specs, scratch=(), limit=40):
    return pl.pallas_call(
        kernel,
        out_shape=out_shape,
        in_specs=specs,
        out_specs=jax.tree.map(lambda _: VM, out_shape),
        scratch_shapes=list(scratch),
        compiler_params=pltpu.CompilerParams(vmem_limit_bytes=limit * MIB),
    )


def sds(shape, dtype):
    return jax.ShapeDtypeStruct(shape, dtype)


def adam_update(embed_table, adam_m, adam_v, row_grad):
    new_moment = beta_first * adam_m + (1.0 - beta_first) * row_grad
    new_second = beta_second * adam_v + (1.0 - beta_second) * row_grad * row_grad
    step_size = new_moment / bias_first / (jnp.sqrt(new_second / bias_second) + adam_eps)
    new_table = embed_table.astype(F32) - learn_rate * step_size
    return (new_table, new_moment, new_second)


def body(
    embed_table,
    adam_m,
    adam_v,
    lengths,
    row_owner,
    row_index,
    proj_weight,
    out_weight,
    norm_gain,
    upstream,
):
    tok_rows = row_index.shape[0]
    groups = lax.axis_size("group")
    seq = lax.axis_size("seq")
    capacity = 2 * tok_rows // groups
    slots = groups * capacity
    tokens = tok_rows * seq
    width = embed_table.shape[1]
    table_rows = embed_table.shape[0]

    col = jnp.arange(4 * PAIR, dtype=jnp.int32)
    source = (col % PAIR) // DH * (4 * DH) + col // PAIR * DH + col % DH
    shuffle = (jnp.arange(4 * PAIR, dtype=jnp.int32)[:, None] == source[None, :]).astype(BF)
    w_own = jnp.dot(proj_weight, shuffle, preferred_element_type=F32).astype(BF)
    w_all = lax.all_gather(w_own, "seq", axis=0)

    owner = row_owner[:, 0]
    hits = (owner[:, None] == jnp.arange(groups, dtype=jnp.int32)[None, :]).astype(BF)
    before = (jnp.arange(tok_rows)[:, None] > jnp.arange(tok_rows)[None, :]).astype(BF)
    ranks = jnp.dot(before, hits, preferred_element_type=F32)
    slot = jnp.sum(ranks * hits.astype(F32), axis=1).astype(jnp.int32)
    pos = owner * capacity + slot
    place = (jnp.arange(slots, dtype=jnp.int32)[:, None] == pos[None, :]).astype(BF)
    requests = jnp.sum(place.astype(F32) * (row_index + 1).astype(F32)[None, :], axis=1)
    asked = lax.all_to_all(
        requests.astype(jnp.int32).reshape(groups, capacity), "group", split_axis=0, concat_axis=0, tiled=True
    ).reshape(slots) - 1
    wanted = (asked[:, None] == jnp.arange(table_rows, dtype=jnp.int32)[None, :]).astype(BF)
    found = jnp.dot(wanted, embed_table, preferred_element_type=F32).astype(BF)
    returned = lax.all_to_all(
        found.reshape(groups, capacity, width), "group", split_axis=0, concat_axis=0, tiled=True
    ).reshape(slots, width)
    embedded = lax.dot_general(place, returned, TN, preferred_element_type=F32).astype(BF)

    emb_all = lax.all_gather(embedded, "seq", axis=0, tiled=True)
    pre = jnp.dot(emb_all, w_own[:, : 3 * PAIR], preferred_element_type=F32)
    qkv = silu_pair(pre)[0].astype(BF)

    att_heads = local_call(attend_kernel, sds((tokens, PAIR), BF), [SM, VM])(lengths, qkv)
    attended = lax.all_to_all(att_heads, "seq", split_axis=0, concat_axis=1, tiled=True)
    layer_out, d_att, d_pre_u = local_call(
        finish_kernel,
        (sds((tok_rows, width), F32), sds((tok_rows, width), BF), sds((tok_rows, width), BF)),
        [VM] * 6,
    )(attended, embedded, w_all[:, :, 3 * PAIR :], out_weight, norm_gain.reshape(1, -1), upstream)
    d_heads = lax.all_to_all(d_att, "seq", split_axis=1, concat_axis=0, tiled=True)
    d_pre_heads = local_call(
        attend_back_kernel,
        sds((tokens, 3 * PAIR), BF),
        [SM, VM, VM, VM],
        [pltpu.VMEM((tokens, PAIR), F32)],
    )(lengths, qkv, pre, d_heads)
    d_qkv = lax.all_to_all(
        d_pre_heads.reshape(seq, tok_rows, 3 * PAIR), "seq", split_axis=0, concat_axis=0, tiled=True
    )
    outgoing = local_call(d_embed_kernel, sds((slots, width), BF), [VM] * 5)(
        pos.reshape(1, -1), d_qkv, d_pre_u, w_all, upstream
    )
    incoming = lax.all_to_all(
        outgoing.reshape(groups, capacity, width), "group", split_axis=0, concat_axis=0, tiled=True
    ).reshape(slots, width)
    partial = lax.dot_general(wanted, incoming, TN, preferred_element_type=F32).astype(BF)
    shares = lax.all_to_all(
        partial.reshape(seq, table_rows // seq, width), "seq", split_axis=0, concat_axis=0, tiled=True
    )
    share = jnp.sum(shares.astype(F32), axis=0).astype(BF)
    row_grad = lax.all_gather(share, "seq", axis=0, tiled=True).astype(F32)
    new_table, new_moment, new_second = adam_update(embed_table, adam_m, adam_v, row_grad)
    return (layer_out, new_table, new_moment, new_second)


def solution(mesh):
    placed = (
        P("group", None),
        P("group", None),
        P("group", None),
        P("group", None),
        P(("group", "seq"), None),
        P(("group", "seq")),
        P(None, "seq"),
        P(),
        P(),
        P(("group", "seq"), None),
    )
    return jax.shard_map(
        body,
        mesh=mesh,
        in_specs=placed,
        out_specs=(P(("group", "seq"), None), P("group", None), P("group", None), P("group", None)),
        check_vma=False,
    )
```

time: 557 us -> 321 us (0.58); the launches traced: 546 us -> 320 us
  local copies, waits for them, and re-layouts: 119 us -> 21.5 us
  blocking collectives: 47.9 us -> 145 us
  matrix products: 109 us -> 12.7 us
  waiting for transfers between devices: 169 us -> 78.4 us
  Pallas kernels: 0 us -> 38.7 us
  other arithmetic: 42.2 us -> 5.1 us
  starting transfers between devices: 30.1 us -> 4.74 us
  loops' own time: 15.3 us -> 0 us
    dot_general x29 -> x6, matrix products: 109 us -> 12.7 us  [the longest x1 6.56 us: body(): pre = jnp.dot(emb_all, w_own[:, :3 * PAIR], preferred_element_type=F32)]
    all_to_all x5 -> x1, waiting for transfers between devices: 108 us -> 20.7 us  [body(): lax.all_to_all(d_pre_heads.reshape(seq, tok_rows, 3 * PAIR), 'seq', split...]
    all_to_all x2 -> x6, blocking collectives: 47.9 us -> 131 us  [the longest x1 35.5 us: body(): lax.all_to_all(outgoing.reshape(groups, capacity, width), 'group', split_...]
    psum x1 -> x0, waiting for transfers between devices: 59.8 us -> none  [body(): row_grad = lax.psum(partial_grad, 'seq')]
    scatter x2 -> x0, local copies, waits for them, and re-layouts: 58 us -> none  [the longest x1 36.3 us: body(): outgoing = jnp.zeros((group_count, capacity, width), jnp.float32).at[dest...]
    all_gather x1 -> x2, waiting for transfers between devices: 0.01 us -> 57.6 us  [the longest x1 34.4 us: body(): emb_all = lax.all_gather(embedded, 'seq', axis=0, tiled=True)]
    pallas_call x0 -> x4, Pallas kernels: none -> 38.7 us  [the longest x1 19.8 us: body(): local_call(attend_back_kernel, sds((tokens, 3 * PAIR), BF), [SM, VM, VM,...]
    all_to_all x5 -> x1, starting transfers between devices: 30.1 us -> 4.66 us  [body(): lax.all_to_all(d_pre_heads.reshape(seq, tok_rows, 3 * PAIR), 'seq', split...]
  transfers between devices with their start and end apart: 7 -> 3, of which waited for: 6 -> 3; matrix products, arithmetic and copies ran while one was open for 8% -> 3% of each run, Pallas kernels for 0% -> 4%
where the time goes in v1:
time: 321 us; the launch traced here: 320 us
  blocking collectives  145 us (45%)
  waiting for transfers between devices  78.4 us (24%)
  Pallas kernels  38.7 us (12%)
  local copies, waits for them, and re-layouts  21.5 us (7%)
  between operations  14.2 us (4%)
  matrix products  12.7 us (4%)
  other arithmetic  5.1 us (2%)
  starting transfers between devices  4.74 us (1%)
    all_to_all x1, blocking collectives, body(): lax.all_to_all(outgoing.reshape(groups, capacity, width), 'group', split_...  35.5 us
    all_gather x1, waiting for transfers between devices, body(): emb_all = lax.all_gather(embedded, 'seq', axis=0, tiled=True)  34.4 us
    all_to_all x1, blocking collectives, body(): lax.all_to_all(found.reshape(groups, capacity, width), 'group', split_axi...  27.4 us
    all_gather x1, waiting for transfers between devices, body(): w_all = lax.all_gather(w_own, 'seq', axis=0)  23.2 us
    all_to_all x1, waiting for transfers between devices, body(): lax.all_to_all(d_pre_heads.reshape(seq, tok_rows, 3 * PAIR), 'seq', split...  20.7 us
    all_to_all x1, blocking collectives, body(): lax.all_to_all(requests.astype(jnp.int32).reshape(groups, capacity), 'gro...  20.5 us
    pallas_call x1, Pallas kernels, body(): local_call(attend_back_kernel, sds((tokens, 3 * PAIR), BF), [SM, VM, VM,...  19.8 us
    all_to_all x1, blocking collectives, body(): lax.all_to_all(att_heads, 'seq', split_axis=0, concat_axis=1, tiled=True)  18.4 us
  transfers between devices with their start and end apart: 3, of which 3 were waited for; matrix products, arithmetic and copies ran while one was open for 3% of the time, Pallas kernels for 4%

profile of v1, /device:TPU:1, one launch (start us, length us, event | category | flops | bytes accessed | tf_op | source)
XLA Modules:
  0.0 320.4 jit_solution(2916325706401086436)
XLA Ops:
  7.2 0.0 copy-start
  7.2 0.0 all-gather.4.cloned.1.call-start
  7.2 1.0 fusion.1
  8.2 0.7 multiply_add_fusion
  8.9 0.7 add_convert_fusion
  9.6 0.2 multiply_reduce_fusion
  9.7 0.1 convert_element_type.79
  9.8 20.5 %all_to_all.64 = s32[32,1,16]{2,1,0:T(1,128)S(1)} all-to-all(s32[32,1,16]{2,1,0:T(1,128)S(1)} %bitcast.46), channel_id=1, replica_groups=mesh['group'=32,'seq'=8] {'group'}, dimensions={0} | all-to-all | bytes 4096 | tf_op jit(solution)/shard_map/all_to_all | solution.py:243
  30.3 0.1 sub.20
  30.4 1.5 convolution_convert_fusion
  31.9 27.4 %all_to_all.65 = bf16[32,16,1024]{2,1,0:T(8,128)(2,1)S(1)} all-to-all(bf16[32,16,1024]{2,1,0:T(8,128)(2,1)S(1)} %bitcast.44), channel_id=1, replica_groups=mesh['group'=32,'seq'=8] {'group'}, dimensions={0} | all-to-all | bytes 2097152 | tf_op jit(solution)/shard_map/all_to_all | solution.py:248
  59.4 1.3 convolution_convert_fusion.3.emb_ref
  60.6 0.0 all-gather.4.cloned.1.call-update
  60.7 0.0 all-gather.6.cloned.1.call-start
  60.7 0.0 copy-done
  60.7 1.7 fusion
  62.5 0.0 all-gather.6.cloned.1.call-update
  62.5 0.0 copy-start.11
  62.5 34.4 %all-gather.4.cloned.1.call-done = bf16[2048,1024]{1,0:T(8,128)(2,1)} async-done(((bf16[256,1024]{1,0:T(8,128)(2,1)}), bf16[2048,1024]{1,0:T(8,128)(2,1)}) %all-gather.4.cloned.1.call-update) | async-done | bytes 4194320 | tf_op jit(solution)/shard_map/all_gather | solution.py:253
  97.0 6.6 %multiply_convert_fusion = (bf16[2048,384]{1,0:T(8,128)(2,1)S(1)}, f32[2048,384]{1,0:T(8,128)}) fusion(bf16[2048,1024]{1,0:T(8,128)(2,1)} %all-gather.4.cloned.1.call-done, bf16[1024,512]{0,1:T(8,128)(2,1)} %fusion), kind=kOutput, calls=%fused_computation | convolution fusion | flops 1614544896 | bytes 9699328 | tf_op jit(solution)/shard_map/dot_general | solution.py:254
  103.5 0.0 copy-done.11
  103.5 11.3 %shard_map.129 = bf16[2048,128]{1,0:T(8,128)(2,1)S(1)} custom-call(s32[1,4]{1,0:T(1,128)S(1)} %copy-done.11, bf16[2048,384]{1,0:T(8,128)(2,1)S(1)} %get-tuple-element.13.qkv_ref), custom_call_target="tpu_custom_call" | custom-call | tf_op jit(solution)/shard_map/pallas_call | solution.py:257
  114.9 18.4 %all_to_all.66 = bf16[8,256,128]{2,1,0:T(8,128)(2,1)S(1)} all-to-all(bf16[8,256,128]{2,1,0:T(8,128)(2,1)S(1)} %bitcast.39), channel_id=1, replica_groups=mesh['group'=32,'seq'=8] {'seq'}, dimensions={0} | all-to-all | bytes 1048576 | tf_op jit(solution)/shard_map/all_to_all | solution.py:258
  133.2 0.9 copy_bitcast_fusion.att_ref
  134.1 23.2 %all-gather.6.cloned.1.call-done = bf16[8192,512]{0,1:T(8,128)(2,1)} async-done(((bf16[1024,512]{0,1:T(8,128)(2,1)}), bf16[8192,512]{0,1:T(8,128)(2,1)}) %all-gather.6.cloned.1.call-update) | async-done | bytes 8388624 | tf_op jit(solution)/shard_map/all_gather | solution.py:233
  157.3 12.0 %copy.26 = bf16[8192,512]{1,0:T(8,128)(2,1)} copy(bf16[8192,512]{0,1:T(8,128)(2,1)} %all-gather.6.cloned.1.call-done) | data formatting | bytes 16777216 | tf_op jit(solution)/shard_map/all_gather | solution.py:233
  169.3 0.0 copy-start.10
  169.3 1.9 slice.9.wu_ref
  171.2 0.1 copy-done.6
  171.3 0.7 copy-done.7
  172.0 3.8 %shard_map.130 = (f32[256,1024]{1,0:T(8,128)}, bf16[256,1024]{1,0:T(8,128)(2,1)S(1)}, bf16[256,1024]{1,0:T(8,128)(2,1)S(1)}) custom-call(bf16[256,1024]{1,0:T(8,128)(2,1)S(1)} %copy-done.6, bf16[256,1024]{1,0:T(8,128)(2,1)S(1)} %copy-done.3, bf16[8,1024,128]{2,1,0:T(8,128)(2,1)S(1)} %slice.9.wu_ref, bf16[1024,1024]{1,0:T(8,128)(2,1)S(1)} %copy-done.7, ...), custom_call_target="tpu_custom_call" | custom-call | tf_op jit(solution)/shard_map/pallas_call | solution.py:259
  175.8 0.1 copy_bitcast_fusion.1
  175.9 12.6 %all_to_all.67 = bf16[256,8,128]{2,0,1:T(8,128)(2,1)S(1)} all-to-all(bf16[256,8,128]{2,0,1:T(8,128)(2,1)S(1)} %copy_bitcast_fusion.1), channel_id=1, replica_groups=mesh['group'=32,'seq'=8] {'seq'}, dimensions={1} | all-to-all | bytes 1048576 | tf_op jit(solution)/shard_map/all_to_all | solution.py:264
  188.5 19.8 %shard_map.131 = bf16[2048,384]{1,0:T(8,128)(2,1)S(1)} custom-call(s32[1,4]{1,0:T(1,128)S(1)} %copy-done.11, bf16[2048,384]{1,0:T(8,128)(2,1)S(1)} %get-tuple-element.13.qkv_ref, f32[2048,384]{1,0:T(8,128)S(1)} %copy-done.4, bf16[2048,128]{1,0:T(8,128)(2,1)S(1)} %bitcast.40), custom_call_target="tpu_custom_call" | custom-call | tf_op jit(solution)/shard_map/pallas_call | solution.py:265
  208.3 1.2 copy-done.2
  209.5 4.7 %all-to-all-start.4 = ((bf16[8,256,384]{2,1,0:T(8,128)(2,1)}), bf16[8,256,384]{2,1,0:T(8,128)(2,1)S(1)}, u32[]{:S(2)}, u32[]{:S(2)}) async-start(bf16[8,256,384]{2,1,0:T(8,128)(2,1)} %bitcast.37), calls=%async_computation.4 | async-start | bytes 3145728 | tf_op jit(solution)/shard_map/all_to_all | solution.py:271
  214.2 20.7 %all-to-all-done.4.dqkv_ref = bf16[8,256,384]{2,1,0:T(8,128)(2,1)S(1)} async-done(((bf16[8,256,384]{2,1,0:T(8,128)(2,1)}), bf16[8,256,384]{2,1,0:T(8,128)(2,1)S(1)}, u32[]{:S(2)}, u32[]{:S(2)}) %all-to-all-start.4) | async-done | bytes 1572896 | tf_op jit(solution)/shard_map/all_to_all | solution.py:271
  234.9 3.4 %copy-done.1 = bf16[8192,512]{1,0:T(8,128)(2,1)S(1)} copy-done((bf16[8192,512]{1,0:T(8,128)(2,1)S(1)}, bf16[8192,512]{1,0:T(8,128)(2,1)}, u32[]{:S(2)}) %copy-start.1) | copy-done | bytes 8388632
  238.3 1.0 copy-done.9
  239.4 3.8 %shard_map.132 = bf16[512,1024]{1,0:T(8,128)(2,1)S(1)} custom-call(s32[1,256]{1,0:T(1,128)S(1)} %bitcast_add_fusion.pos_ref, bf16[8,256,384]{2,1,0:T(8,128)(2,1)S(1)} %all-to-all-done.4.dqkv_ref, bf16[256,1024]{1,0:T(8,128)(2,1)S(1)} %copy-done.9, bf16[8,1024,512]{2,1,0:T(8,128)(2,1)S(1)} %bitcast.36, bf16[256,1024]{1,0:T(8,128)(2,1)S(1)} %copy-done.5), custom_call_target="tpu_custom_call" | custom-call | tf_op jit(solution)/shard_map/pallas_call | solution.py:274
  243.1 0.0 copy-start.12
  243.1 0.0 copy-start.13
  243.2 35.5 %all_to_all.68 = bf16[32,16,1024]{2,1,0:T(8,128)(2,1)S(1)} all-to-all(bf16[32,16,1024]{2,1,0:T(8,128)(2,1)S(1)} %bitcast.38), channel_id=1, replica_groups=mesh['group'=32,'seq'=8] {'group'}, dimensions={0} | all-to-all | bytes 2097152 | tf_op jit(solution)/shard_map/all_to_all | solution.py:277
  278.7 0.6 convolution_convert_fusion.2
  279.2 16.8 %all_to_all.69 = bf16[8,32,1024]{2,1,0:T(8,128)(2,1)S(1)} all-to-all(bf16[8,32,1024]{2,1,0:T(8,128)(2,1)S(1)} %bitcast.45), channel_id=1, replica_groups=mesh['group'=32,'seq'=8] {'seq'}, dimensions={0} | all-to-all | bytes 1048576 | tf_op jit(solution)/shard_map/all_to_all | solution.py:281
  296.0 0.1 reduce_sum.32
  296.1 14.0 %all_gather.15 = bf16[256,1024]{1,0:T(8,128)(2,1)S(1)} all-gather(bf16[32,1024]{1,0:T(8,128)(2,1)S(1)} %reduce_sum.32), channel_id=1, replica_groups=mesh['group'=32,'seq'=8] {'seq'}, dimensions={0}, use_global_device_ids=true | all-gather | bytes 589824 | tf_op jit(solution)/shard_map/all_gather | solution.py:285
  310.1 3.4 %multiply_subtract_fusion = (f32[256,1024]{1,0:T(8,128)}, f32[256,1024]{1,0:T(8,128)}, f32[256,1024]{1,0:T(8,128)}) fusion(bf16[256,1024]{1,0:T(8,128)(2,1)S(1)} %copy-done.12, bf16[256,1024]{1,0:T(8,128)(2,1)S(1)} %all_gather.15, f32[256,1024]{1,0:T(8,128)S(1)} %copy-done.13, f32[256,1024]{1,0:T(8,128)} %param.12), kind=kLoop, calls=%fused_computation.12 | loop fusion | flops 3932160 | bytes 6291456 | tf_op jit(solution)/shard_map/sub | solution.py:204
  (23 shorter events, 0.1 us)
Async XLA Ops:
  7.2 53.6 %copy-start = (bf16[1024,512]{1,0:T(8,128)(2,1)S(1)}, bf16[1024,512]{1,0:T(8,128)(2,1)}, u32[]{:S(2)}) copy-start(bf16[1024,512]{1,0:T(8,128)(2,1)} %param.16) | copy-start | bytes 3145732
  7.2 89.8 %all-gather.4.cloned.1.call-start = ((), (), s32[]{:S(2)}) async-start(), calls=%async_computation.7 | async-start | bytes 4718592 | tf_op jit(solution)/shard_map/all_gather | solution.py:253
  60.7 96.6 %all-gather.6.cloned.1.call-start = ((), (), s32[]{:S(2)}) async-start(), calls=%async_computation.8 | async-start | bytes 9437184 | tf_op jit(solution)/shard_map/all_gather | solution.py:233
  62.5 41.0 %copy-start.11 = (s32[1,4]{1,0:T(1,128)S(1)}, s32[1,4]{1,0:T(1,128)}, u32[]{:S(2)}) copy-start(s32[1,4]{1,0:T(1,128)} %len_ref.3) | copy-start | bytes 52
  169.2 1.9 copy-start.3
  169.2 1.9 copy-start.5
  169.3 2.0 copy-start.6
  169.3 2.7 copy-start.7
  169.3 2.7 copy-start.10
  172.0 16.5 %copy-start.4 = (f32[2048,384]{1,0:T(8,128)S(1)}, f32[2048,384]{1,0:T(8,128)}, u32[]{:S(2)}) copy-start(f32[2048,384]{1,0:T(8,128)} %get-tuple-element.14.pre_ref) | copy-start | bytes 9437188
  175.8 12.7 %copy-start.8 = (bf16[256,1024]{1,0:T(8,128)(2,1)}, bf16[256,1024]{1,0:T(8,128)(2,1)S(1)}, u32[]{:S(2)}) copy-start(bf16[256,1024]{1,0:T(8,128)(2,1)S(1)} %get-tuple-element.9.dpu_ref) | copy-start | bytes 1572868
  208.3 1.2 copy-start.2
  209.5 4.7 %copy-start.14 = (s32[256,1]{0,1:T(1,128)S(1)}, s32[256,1]{0,1:T(1,128)}, u32[]{:S(2)}) copy-start(s32[256,1]{0,1:T(1,128)} %param.14) | copy-start | bytes 3076
  209.5 25.4 %all-to-all-start.4 = ((bf16[8,256,384]{2,1,0:T(8,128)(2,1)}), bf16[8,256,384]{2,1,0:T(8,128)(2,1)S(1)}, u32[]{:S(2)}, u32[]{:S(2)}) async-start(bf16[8,256,384]{2,1,0:T(8,128)(2,1)} %bitcast.37), calls=%async_computation.4 | async-start | bytes 3145728 | tf_op jit(solution)/shard_map/all_to_all | solution.py:271
  234.9 3.4 %copy-start.1 = (bf16[8192,512]{1,0:T(8,128)(2,1)S(1)}, bf16[8192,512]{1,0:T(8,128)(2,1)}, u32[]{:S(2)}) copy-start(bf16[8192,512]{1,0:T(8,128)(2,1)} %copy.26) | copy-start | bytes 25165828
  238.3 1.0 copy-start.9
  243.1 67.0 %copy-start.12 = (bf16[256,1024]{1,0:T(8,128)(2,1)S(1)}, bf16[256,1024]{1,0:T(8,128)(2,1)}, u32[]{:S(2)}) copy-start(bf16[256,1024]{1,0:T(8,128)(2,1)} %param.10) | copy-start | bytes 1572868
  243.1 67.0 %copy-start.13 = (f32[256,1024]{1,0:T(8,128)S(1)}, f32[256,1024]{1,0:T(8,128)}, u32[]{:S(2)}) copy-start(f32[256,1024]{1,0:T(8,128)} %param.11) | copy-start | bytes 3145732
Sparse Core Ops, SparseCore 0:
  60.8 36.1 all-gather.3
  99.4 57.8 all-gather.5

commit v2 on v1

--- a/solution.py
+++ b/solution.py
@@ -139,42 +139,364 @@
         finish_part(rows, 2, dv)
 
 
-def finish_kernel(att_ref, emb_ref, wu_ref, wo_ref, gain_ref, up_ref, layer_ref, datt_ref, dpu_ref):
-    seq = wu_ref.shape[0]
+def shuffle_kernel(w_ref, out_ref):
+    size = w_ref.shape[1]
+    row = lax.broadcasted_iota(jnp.int32, (size, size), 0)
+    col = lax.broadcasted_iota(jnp.int32, (size, size), 1)
+    lane = lax.rem(col, PAIR)
+    source = lax.div(lane, DH) * (4 * DH) + lax.div(col, PAIR) * DH + lax.rem(lane, DH)
+    move = jnp.where(row == source, 1.0, 0.0).astype(BF)
+    out_ref[...] = mm(w_ref[...], move).astype(BF)
+
+
+def group_peers(k, groups):
+    depth = min(8, groups)
+    lines = groups // depth
+    me = lax.axis_index("group")
+    y, z = lax.div(me, depth), lax.rem(me, depth)
+    dy, dz = lax.div(k, depth), lax.rem(k * 3, depth)
+    to = lax.rem(y + dy, lines) * depth + lax.rem(z + dz, depth)
+    return to
+
+
+def seq_peer(k, seq):
+    return lax.rem(lax.axis_index("seq") + k, seq)
+
+
+def send(src, dst, out_sem, in_sem, **where):
+    return pltpu.make_async_remote_copy(
+        src_ref=src,
+        dst_ref=dst,
+        send_sem=out_sem,
+        recv_sem=in_sem,
+        device_id=where,
+        device_id_type=pl.DeviceIdType.MESH,
+    )
+
+
+def greet(groups, seq_steps, seq):
+    barrier = pltpu.get_barrier_semaphore()
+
+    @pl.loop(1, groups)
+    def _(k):
+        pl.semaphore_signal(
+            barrier, inc=1, device_id={"group": group_peers(k, groups)}, device_id_type=pl.DeviceIdType.MESH
+        )
+
+    for peer in seq_steps:
+        pl.semaphore_signal(barrier, inc=1, device_id={"seq": peer}, device_id_type=pl.DeviceIdType.MESH)
+    return barrier, groups - 1 + len(seq_steps)
+
+
+def slot_places(owner, slots, groups):
+    rows = owner.shape[1]
+    hits = lax.broadcasted_iota(jnp.int32, (groups, rows), 0) == owner
+    earlier = lax.broadcasted_iota(jnp.int32, (rows, rows), 0) < lax.broadcasted_iota(jnp.int32, (rows, rows), 1)
+    count = mm(jnp.where(hits, 1.0, 0.0).astype(BF), jnp.where(earlier, 1.0, 0.0).astype(BF))
+    slot = jnp.sum(jnp.where(hits, count, 0.0), axis=0, keepdims=True).astype(jnp.int32)
+    pos = owner * (slots // groups) + slot
+    return jnp.where(lax.broadcasted_iota(jnp.int32, (slots, rows), 0) == pos, 1.0, 0.0).astype(BF)
+
+
+def fetch_kernel(
+    groups, seq, owner_ref, index_ref, table_ref, w_ref,
+    emb_ref, pre_ref, qkv_ref, wanted_ref, place_ref,
+    ask_out, ask_in, row_out, row_in, ring, ask_s, ask_r, row_s, row_r, ring_s, ring_r,
+):
+    chunks, slots, cut = row_out.shape
+    rows = owner_ref.shape[1]
+    cap = slots // groups
+    table_rows = table_ref.shape[0]
+    wide = 3 * PAIR
+    g, s = lax.axis_index("group"), lax.axis_index("seq")
+    chips = seq // 2
+    x, core = lax.div(s, 2), lax.rem(s, 2)
+    flip = 1 - 2 * core
+    right = lax.rem(x + 1, chips) * 2 + core
+    left = lax.rem(x + chips - 1, chips) * 2 + core
+    across = lax.rem(x + 2, chips) * 2 + core
+    sib = s + flip
+
+    barrier, greeted = greet(groups, [sib, right, left], seq)
+    place_ref[...] = slot_places(owner_ref[...], slots, groups)
+    index = jnp.broadcast_to((index_ref[...] + 1).astype(F32), (PAIR, rows)).astype(BF)
+    ask_out[...] = mm(place_ref[...], index, NT).astype(BF)
+    pl.semaphore_wait(barrier, greeted)
+
+    mine = pl.ds(pl.multiple_of(g * cap, cap), cap)
+
+    def ask(k):
+        to = group_peers(k, groups)
+        return send(
+            ask_out.at[pl.ds(pl.multiple_of(to * cap, cap), cap)], ask_in.at[mine], ask_s.at[k], ask_r.at[k], group=to
+        )
+
+    def give(c, k):
+        to = group_peers(k, groups)
+        return send(
+            row_out.at[c, pl.ds(pl.multiple_of(to * cap, cap), cap)], row_in.at[c, mine],
+            row_s.at[c, k], row_r.at[c, k], group=to,
+        )
+
+    @pl.loop(1, groups)
+    def _(k):
+        ask(k).start()
+
+    ask_in[mine] = ask_out[mine]
+
+    @pl.loop(1, groups)
+    def _(k):
+        ask(k).wait()
+
+    wanted = ask_in[...].astype(F32).astype(jnp.int32)
+    for part in range(table_rows // PAIR):
+        lane = lax.broadcasted_iota(jnp.int32, wanted.shape, 1) + (part * PAIR + 1)
+        wanted_ref[:, part * PAIR : (part + 1) * PAIR] = jnp.where(wanted == lane, 1.0, 0.0).astype(BF)
+
+    for c in range(chunks):
+        row_out[c] = mm(wanted_ref[...], table_ref[:, c * cut : (c + 1) * cut]).astype(BF)
+
+        @pl.loop(1, groups)
+        def _(k):
+            give(c, k).start()
+
+        row_in[c, mine] = row_out[c, mine]
+
+    half = rows // 2
+
+    def hop(c, op, block, to, low=0, size=rows):
+        view = ring.at[c, block, pl.ds(low, size)]
+        return send(view, view, ring_s.at[c, op], ring_r.at[c, op], seq=to)
+
+    def project(c, block):
+        at = pl.ds(pl.multiple_of(block * rows, rows), rows)
+        val = mm(ring[c, block], w_ref[c * cut : (c + 1) * cut, :wide])
+        if c > 0:
+            val = val + pre_ref[at]
+        pre_ref[at] = val
+        if c == chunks - 1:
+            qkv_ref[at] = silu_pair(val)[0].astype(BF)
+
+    for c in range(chunks):
+
+        @pl.loop(1, groups)
+        def _(k):
+            give(c, k).wait()
+
+        block = mm(place_ref[...], row_in[c], TN).astype(BF)
+        emb_ref[:, c * cut : (c + 1) * cut] = block
+        ring[c, s] = block
+        hop(c, 1, s, right).start()
+        hop(c, 2, s, left).start()
+        hop(c, 0, s, sib).start()
+        project(c, s)
+        hop(c, 1, left, right).wait_recv()
+        hop(c, 3, left, right, 0, half).start()
+        hop(c, 4, left, sib).start()
+        hop(c, 2, right, left).wait_recv()
+        hop(c, 5, right, left, half, half).start()
+        hop(c, 6, right, sib).start()
+        project(c, left)
+        project(c, right)
+        hop(c, 0, sib, sib).wait_recv()
+        project(c, sib)
+        hop(c, 3, across, right, 0, half).wait_recv()
+        hop(c, 7, across, sib, 0, half).start()
+        hop(c, 5, across, left, half, half).wait_recv()
+        hop(c, 8, across, sib, half, half).start()
+        project(c, across)
+        hop(c, 4, left + flip, sib).wait_recv()
+        project(c, left + flip)
+        hop(c, 6, right + flip, sib).wait_recv()
+        project(c, right + flip)
+        hop(c, 7, across + flip, sib, 0, half).wait_recv()
+        hop(c, 8, across + flip, sib, half, half).wait_recv()
+        project(c, across + flip)
+
+    for c in range(chunks):
+        hop(c, 1, s, right).wait_send()
+        hop(c, 2, s, left).wait_send()
+        hop(c, 0, s, sib).wait_send()
+        hop(c, 3, left, right, 0, half).wait_send()
+        hop(c, 4, left, sib).wait_send()
+        hop(c, 5, right, left, half, half).wait_send()
+        hop(c, 6, right, sib).wait_send()
+        hop(c, 7, across, sib, 0, half).wait_send()
+        hop(c, 8, across, sib, half, half).wait_send()
+
+
+def middle_kernel(
+    seq, att_ref, emb_ref, w_ref, wo_ref, gain_ref, up_ref,
+    layer_ref, dheads_ref, dpu_ref,
+    wu, att_in, datt_out, datt_in, d_mixed, pre_u, w_s, att_s, att_r, datt_s, datt_r,
+):
+    rows, width = emb_ref.shape
+    s = lax.axis_index("seq")
+    order = [4, 3, 5, 2, 6, 1, 7]
+
+    def load(b):
+        return pltpu.make_async_copy(
+            w_ref.at[pl.ds(b * width, width), 3 * PAIR : 4 * PAIR], wu.at[b], w_s.at[b]
+        )
+
+    for b in range(seq):
+        load(b).start()
+    barrier, greeted = greet(1, [seq_peer(k, seq) for k in range(1, seq)], seq)
+    pl.semaphore_wait(barrier, greeted)
+
+    def hand(k):
+        to = seq_peer(k, seq)
+        return send(
+            att_ref.at[pl.ds(pl.multiple_of(to * rows, rows), rows)], att_in.at[s], att_s.at[k], att_r.at[k], seq=to
+        )
+
+    def back(k):
+        to = seq_peer(k, seq)
+        return send(datt_out.at[to], datt_in.at[s], datt_s.at[k], datt_r.at[k], seq=to)
+
+    for k in order:
+        hand(k).start()
+    att_in[s] = att_ref[pl.ds(pl.multiple_of(s * rows, rows), rows)]
+    d_mixed[...] = mm(up_ref[...], wo_ref[...], NT)
     emb = emb_ref[...]
-    d_mixed = mm(up_ref[...], wo_ref[...], NT)
-    x = att_ref[...].astype(F32)
-    center = x - jnp.mean(x, axis=-1, keepdims=True)
+    for b in range(seq):
+        load(b).wait()
+        pre_u[:, b * PAIR : (b + 1) * PAIR] = mm(emb, wu[b])
+    for k in order:
+        hand(k).wait()
+
+    att = jnp.concatenate([att_in[b] for b in range(seq)], axis=1).astype(F32)
+    center = att - jnp.mean(att, axis=-1, keepdims=True)
     spread = jnp.mean(center * center, axis=-1, keepdims=True)
     r = lax.rsqrt(spread + norm_eps)
     xhat = center * r
     gain = gain_ref[...]
     normed = xhat * gain
-    pre_u = jnp.concatenate([mm(emb, wu_ref[s]) for s in range(seq)], axis=1)
-    act_u, slope_u = silu_pair(pre_u)
+    act_u, slope_u = silu_pair(pre_u[...])
     u = act_u.astype(BF).astype(F32)
-    mixed = (normed * u).astype(BF)
-    layer_ref[...] = emb.astype(F32) + mm(mixed, wo_ref[...])
-    dpu_ref[...] = ((d_mixed * normed).astype(BF).astype(F32) * slope_u).astype(BF)
-    gx = d_mixed * u * gain
+    d_mix = d_mixed[...]
+    gx = d_mix * u * gain
     datt = r * (
         gx
         - jnp.mean(gx, axis=-1, keepdims=True)
         - xhat * jnp.mean(gx * xhat, axis=-1, keepdims=True)
     )
-    datt_ref[...] = datt.astype(BF)
-
-
-def d_embed_kernel(pos_ref, dqkv_ref, dpu_ref, w_ref, up_ref, out_ref):
-    seq = w_ref.shape[0]
-    d_emb = up_ref[...].astype(F32)
-    for s in range(seq):
-        d_emb = d_emb + mm(dqkv_ref[s], w_ref[s][:, : 3 * PAIR], NT)
-        d_emb = d_emb + mm(dpu_ref[:, s * PAIR : (s + 1) * PAIR], w_ref[s][:, 3 * PAIR :], NT)
-    slots = out_ref.shape[0]
-    slot = lax.broadcasted_iota(jnp.int32, (slots, pos_ref.shape[1]), 0)
-    place = jnp.where(slot == pos_ref[...], 1.0, 0.0).astype(BF)
-    out_ref[...] = mm(place, d_emb.astype(BF)).astype(BF)
+    datt = datt.astype(BF)
+    for b in range(seq):
+        datt_out[b] = datt[:, b * PAIR : (b + 1) * PAIR]
+    for k in order:
+        back(k).start()
+    datt_in[s] = datt_out[s]
+    dpu = ((d_mix * normed).astype(BF).astype(F32) * slope_u).astype(BF)
+    for b in range(seq):
+        dpu_ref[b] = dpu[:, b * PAIR : (b + 1) * PAIR]
+    mixed = (normed * u).astype(BF)
+    layer_ref[...] = emb.astype(F32) + mm(mixed, wo_ref[...])
+    for k in order:
+        back(k).wait()
+    dheads_ref[...] = datt_in[...]
+
+
+def back_kernel(
+    groups, seq, dqkv_ref, dpu_ref, place_ref, wanted_ref, w_ref, up_ref,
+    grad_ref,
+    w_vm, d_in, row_out, row_in, part, part_f, part_in, share, share_in,
+    w_s, d_s, d_r, row_s, row_r, part_s, part_r, share_s, share_r,
+):
+    chunks, slots, cut = row_out.shape
+    rows, width = up_ref.shape
+    cap = slots // groups
+    wide = 3 * PAIR
+    own = grad_ref.shape[0] // seq
+    g, s = lax.axis_index("group"), lax.axis_index("seq")
+    order = [4, 3, 5, 2, 6, 1, 7]
+
+    def load(b):
+        return pltpu.make_async_copy(w_ref.at[pl.ds(b * width, width)], w_vm.at[b], w_s.at[b])
+
+    for b in range(seq):
+        load(b).start()
+    barrier, greeted = greet(groups, [seq_peer(k, seq) for k in range(1, seq)], seq)
+    for b in range(seq):
+        d_in[b, :, wide:] = dpu_ref[b]
+    d_in[s, :, :wide] = dqkv_ref[pl.ds(pl.multiple_of(s * rows, rows), rows)]
+    pl.semaphore_wait(barrier, greeted)
+
+    def hand(k):
+        to = seq_peer(k, seq)
+        return send(
+            dqkv_ref.at[pl.ds(pl.multiple_of(to * rows, rows), rows)], d_in.at[s, :, 0:wide],
+            d_s.at[k], d_r.at[k], seq=to,
+        )
+
+    mine = pl.ds(pl.multiple_of(g * cap, cap), cap)
+
+    def give(c, k):
+        to = group_peers(k, groups)
+        return send(
+            row_out.at[c, pl.ds(pl.multiple_of(to * cap, cap), cap)], row_in.at[c, mine],
+            row_s.at[c, k], row_r.at[c, k], group=to,
+        )
+
+    def spread(c, k):
+        to = seq_peer(k, seq)
+        return send(part.at[c, to], part_in.at[c, s], part_s.at[c, k], part_r.at[c, k], seq=to)
+
+    def copy_share(c, k):
+        to = seq_peer(k, seq)
+        return send(share.at[c], share_in.at[c, s], share_s.at[c, k], share_r.at[c, k], seq=to)
+
+    for k in order:
+        hand(k).start()
+    for b in range(seq):
+        load(b).wait()
+
+    for c in range(chunks):
+        cols = slice(c * cut, (c + 1) * cut)
+        total = up_ref[:, cols].astype(F32)
+        for k in [0, 7, 1, 6, 2, 5, 3, 4]:
+            b = lax.rem(s + seq - k, seq)
+            if c == 0 and k > 0:
+                hand(k).wait_recv()
+            total = total + mm(d_in[b], w_vm[b, cols, :], NT)
+        row_out[c] = mm(place_ref[...], total.astype(BF)).astype(BF)
+
+        @pl.loop(1, groups)
+        def _(k):
+            give(c, k).start()
+
+        row_in[c, mine] = row_out[c, mine]
+
+    for c in range(chunks):
+
+        @pl.loop(1, groups)
+        def _(k):
+            give(c, k).wait()
+
+        sums = mm(wanted_ref[...], row_in[c], TN)
+        for b in range(seq):
+            part[c, b] = sums[b * own : (b + 1) * own].astype(BF)
+            part_f[b] = sums[b * own : (b + 1) * own]
+        for k in order:
+            spread(c, k).start()
+        total = part_f[s]
+        for k in range(1, seq):
+            spread(c, k).wait_recv()
+            total = total + part_in[c, lax.rem(s + seq - k, seq)].astype(F32)
+        share[c] = total
+        for k in order:
+            copy_share(c, k).start()
+        share_in[c, s] = total
+
+    for c in range(chunks):
+        for k in order:
+            copy_share(c, k).wait()
+        for b in range(seq):
+            grad_ref[b * own : (b + 1) * own, c * cut : (c + 1) * cut] = share_in[c, b]
+        for k in order:
+            spread(c, k).wait_send()
+    for k in order:
+        hand(k).wait_send()
 
 
 VM = pl.BlockSpec(memory_space=pltpu.VMEM)
@@ -191,6 +513,24 @@
         scratch_shapes=list(scratch),
         compiler_params=pltpu.CompilerParams(vmem_limit_bytes=limit * MIB),
     )
+
+
+def remote_call(kernel, ident, out_shape, specs, scratch, limit=48):
+    return pl.pallas_call(
+        kernel,
+        out_shape=out_shape,
+        in_specs=specs,
+        out_specs=jax.tree.map(lambda _: VM, out_shape),
+        scratch_shapes=list(scratch),
+        compiler_params=pltpu.CompilerParams(
+            collective_id=ident, has_side_effects=True, vmem_limit_bytes=limit * MIB
+        ),
+    )
+
+
+ANY = pl.BlockSpec(memory_space=pl.ANY)
+CHUNKS = 2
+DMA = pltpu.SemaphoreType.DMA
 
 
 def sds(shape, dtype):
@@ -226,63 +566,94 @@
     width = embed_table.shape[1]
     table_rows = embed_table.shape[0]
 
-    col = jnp.arange(4 * PAIR, dtype=jnp.int32)
-    source = (col % PAIR) // DH * (4 * DH) + col // PAIR * DH + col % DH
-    shuffle = (jnp.arange(4 * PAIR, dtype=jnp.int32)[:, None] == source[None, :]).astype(BF)
-    w_own = jnp.dot(proj_weight, shuffle, preferred_element_type=F32).astype(BF)
-    w_all = lax.all_gather(w_own, "seq", axis=0)
-
-    owner = row_owner[:, 0]
-    hits = (owner[:, None] == jnp.arange(groups, dtype=jnp.int32)[None, :]).astype(BF)
-    before = (jnp.arange(tok_rows)[:, None] > jnp.arange(tok_rows)[None, :]).astype(BF)
-    ranks = jnp.dot(before, hits, preferred_element_type=F32)
-    slot = jnp.sum(ranks * hits.astype(F32), axis=1).astype(jnp.int32)
-    pos = owner * capacity + slot
-    place = (jnp.arange(slots, dtype=jnp.int32)[:, None] == pos[None, :]).astype(BF)
-    requests = jnp.sum(place.astype(F32) * (row_index + 1).astype(F32)[None, :], axis=1)
-    asked = lax.all_to_all(
-        requests.astype(jnp.int32).reshape(groups, capacity), "group", split_axis=0, concat_axis=0, tiled=True
-    ).reshape(slots) - 1
-    wanted = (asked[:, None] == jnp.arange(table_rows, dtype=jnp.int32)[None, :]).astype(BF)
-    found = jnp.dot(wanted, embed_table, preferred_element_type=F32).astype(BF)
-    returned = lax.all_to_all(
-        found.reshape(groups, capacity, width), "group", split_axis=0, concat_axis=0, tiled=True
-    ).reshape(slots, width)
-    embedded = lax.dot_general(place, returned, TN, preferred_element_type=F32).astype(BF)
-
-    emb_all = lax.all_gather(embedded, "seq", axis=0, tiled=True)
-    pre = jnp.dot(emb_all, w_own[:, : 3 * PAIR], preferred_element_type=F32)
-    qkv = silu_pair(pre)[0].astype(BF)
+    cut = width // CHUNKS
+
+    w_own = local_call(shuffle_kernel, sds(proj_weight.shape, BF), [VM])(proj_weight)
+    w_all = lax.all_gather(w_own, "seq", axis=0, tiled=True)
+
+    embedded, pre, qkv, wanted, place = remote_call(
+        functools.partial(fetch_kernel, groups, seq),
+        1,
+        (
+            sds((tok_rows, width), BF),
+            sds((tokens, 3 * PAIR), F32),
+            sds((tokens, 3 * PAIR), BF),
+            sds((slots, table_rows), BF),
+            sds((slots, tok_rows), BF),
+        ),
+        [VM] * 4,
+        [
+            pltpu.VMEM((slots, PAIR), BF),
+            pltpu.VMEM((slots, PAIR), BF),
+            pltpu.VMEM((CHUNKS, slots, cut), BF),
+            pltpu.VMEM((CHUNKS, slots, cut), BF),
+            pltpu.VMEM((CHUNKS, seq, tok_rows, cut), BF),
+            DMA((groups,)),
+            DMA((groups,)),
+            DMA((CHUNKS, groups)),
+            DMA((CHUNKS, groups)),
+            DMA((CHUNKS, 9)),
+            DMA((CHUNKS, 9)),
+        ],
+    )(row_owner.reshape(1, -1), row_index.reshape(1, -1), embed_table, w_own)
 
     att_heads = local_call(attend_kernel, sds((tokens, PAIR), BF), [SM, VM])(lengths, qkv)
-    attended = lax.all_to_all(att_heads, "seq", split_axis=0, concat_axis=1, tiled=True)
-    layer_out, d_att, d_pre_u = local_call(
-        finish_kernel,
-        (sds((tok_rows, width), F32), sds((tok_rows, width), BF), sds((tok_rows, width), BF)),
-        [VM] * 6,
-    )(attended, embedded, w_all[:, :, 3 * PAIR :], out_weight, norm_gain.reshape(1, -1), upstream)
-    d_heads = lax.all_to_all(d_att, "seq", split_axis=1, concat_axis=0, tiled=True)
+    layer_out, d_heads, d_pre_u = remote_call(
+        functools.partial(middle_kernel, seq),
+        2,
+        (
+            sds((tok_rows, width), F32),
+            sds((seq, tok_rows, PAIR), BF),
+            sds((seq, tok_rows, PAIR), BF),
+        ),
+        [VM, VM, ANY, VM, VM, VM],
+        [
+            pltpu.VMEM((seq, width, PAIR), BF),
+            pltpu.VMEM((seq, tok_rows, PAIR), BF),
+            pltpu.VMEM((seq, tok_rows, PAIR), BF),
+            pltpu.VMEM((seq, tok_rows, PAIR), BF),
+            pltpu.VMEM((tok_rows, width), F32),
+            pltpu.VMEM((tok_rows, width), F32),
+            DMA((seq,)),
+            DMA((seq,)),
+            DMA((seq,)),
+            DMA((seq,)),
+            DMA((seq,)),
+        ],
+    )(att_heads, embedded, w_all, out_weight, norm_gain.reshape(1, -1), upstream)
     d_pre_heads = local_call(
         attend_back_kernel,
         sds((tokens, 3 * PAIR), BF),
         [SM, VM, VM, VM],
         [pltpu.VMEM((tokens, PAIR), F32)],
-    )(lengths, qkv, pre, d_heads)
-    d_qkv = lax.all_to_all(
-        d_pre_heads.reshape(seq, tok_rows, 3 * PAIR), "seq", split_axis=0, concat_axis=0, tiled=True
-    )
-    outgoing = local_call(d_embed_kernel, sds((slots, width), BF), [VM] * 5)(
-        pos.reshape(1, -1), d_qkv, d_pre_u, w_all, upstream
-    )
-    incoming = lax.all_to_all(
-        outgoing.reshape(groups, capacity, width), "group", split_axis=0, concat_axis=0, tiled=True
-    ).reshape(slots, width)
-    partial = lax.dot_general(wanted, incoming, TN, preferred_element_type=F32).astype(BF)
-    shares = lax.all_to_all(
-        partial.reshape(seq, table_rows // seq, width), "seq", split_axis=0, concat_axis=0, tiled=True
-    )
-    share = jnp.sum(shares.astype(F32), axis=0).astype(BF)
-    row_grad = lax.all_gather(share, "seq", axis=0, tiled=True).astype(F32)
+    )(lengths, qkv, pre, d_heads.reshape(tokens, PAIR))
+    own = table_rows // seq
+    row_grad = remote_call(
+        functools.partial(back_kernel, groups, seq),
+        3,
+        sds((table_rows, width), F32),
+        [VM, VM, VM, VM, ANY, VM],
+        [
+            pltpu.VMEM((seq, width, 4 * PAIR), BF),
+            pltpu.VMEM((seq, tok_rows, 4 * PAIR), BF),
+            pltpu.VMEM((CHUNKS, slots, cut), BF),
+            pltpu.VMEM((CHUNKS, slots, cut), BF),
+            pltpu.VMEM((CHUNKS, seq, own, cut), BF),
+            pltpu.VMEM((seq, own, cut), F32),
+            pltpu.VMEM((CHUNKS, seq, own, cut), BF),
+            pltpu.VMEM((CHUNKS, own, cut), F32),
+            pltpu.VMEM((CHUNKS, seq, own, cut), F32),
+            DMA((seq,)),
+            DMA((seq,)),
+            DMA((seq,)),
+            DMA((CHUNKS, groups)),
+            DMA((CHUNKS, groups)),
+            DMA((CHUNKS, seq)),
+            DMA((CHUNKS, seq)),
+            DMA((CHUNKS, seq)),
+            DMA((CHUNKS, seq)),
+        ],
+    )(d_pre_heads, d_pre_u, place, wanted, w_all, upstream)
     new_table, new_moment, new_second = adam_update(embed_table, adam_m, adam_v, row_grad)
     return (layer_out, new_table, new_moment, new_second)
 

time: 321 us -> 224 us (0.70)
  Pallas kernels: 38.7 us -> 200 us
  blocking collectives: 145 us -> 0 us
  waiting for transfers between devices: 78.4 us -> 0.04 us
  local copies, waits for them, and re-layouts: 21.5 us -> 6.4 us
  matrix products: 12.7 us -> 0 us
  starting transfers between devices: 4.74 us -> 0.04 us
    pallas_call x2 -> x4, Pallas kernels: 7.6 us -> 169 us  [the longest x1 78.8 us: body(): remote_call(functools.partial(fetch_kernel, groups, seq), 1, (sds((tok_ro...]
    all_to_all x6 -> x0, blocking collectives: 131 us -> none  [the longest x1 35.5 us: body(): lax.all_to_all(outgoing.reshape(groups, capacity, width), 'group', split_...]
    all_gather x2 -> x1, waiting for transfers between devices: 57.6 us -> 0.02 us  [body(): w_all = lax.all_gather(w_own, 'seq', axis=0, tiled=True)]
    all_to_all x1 -> x0, waiting for transfers between devices: 20.7 us -> none  [body(): lax.all_to_all(d_pre_heads.reshape(seq, tok_rows, 3 * PAIR), 'seq', split...]
    all_gather x1 -> x0, blocking collectives: 14 us -> none  [body(): row_grad = lax.all_gather(share, 'seq', axis=0, tiled=True).astype(F32)]
    dot_general x6 -> x0, matrix products: 12.7 us -> none  [the longest x1 6.56 us: body(): pre = jnp.dot(emb_all, w_own[:, :3 * PAIR], preferred_element_type=F32)]
    all_gather x1 -> x0, local copies, waits for them, and re-layouts: 12 us -> none  [body(): w_all = lax.all_gather(w_own, 'seq', axis=0)]
    all_to_all x1 -> x0, starting transfers between devices: 4.66 us -> none  [body(): lax.all_to_all(d_pre_heads.reshape(seq, tok_rows, 3 * PAIR), 'seq', split...]
  transfers between devices with their start and end apart: 3 -> 1, of which waited for: 3 -> 0; matrix products, arithmetic and copies ran while one was open for 3% -> 0% of each run, Pallas kernels for 4% -> 40%
where the time goes in v2:
time: 224 us; the launch traced here: 223 us
  Pallas kernels  200 us (89%)
  between operations  14.2 us (6%)
  local copies, waits for them, and re-layouts  6.4 us (3%)
  other arithmetic  2.28 us (1%)
    pallas_call x1, Pallas kernels, body(): remote_call(functools.partial(fetch_kernel, groups, seq), 1, (sds((tok_ro...  78.8 us
    pallas_call x1, Pallas kernels, body(): remote_call(functools.partial(back_kernel, groups, seq), 3, sds((table_ro...  70.3 us
    pallas_call x1, Pallas kernels, body(): local_call(attend_back_kernel, sds((tokens, 3 * PAIR), BF), [SM, VM, VM,...  19.9 us
    pallas_call x1, Pallas kernels, body(): remote_call(functools.partial(middle_kernel, seq), 2, (sds((tok_rows, wid...  18.3 us
    pallas_call x1, Pallas kernels, body(): local_call(attend_kernel, sds((tokens, PAIR), BF), [SM, VM])(lengths, qkv)  11.3 us
    unnamed x31, local copies, waits for them, and re-layouts  6.4 us
  transfers between devices with their start and end apart: 1, of which 0 were waited for; matrix products, arithmetic and copies ran while one was open for 0% of the time, Pallas kernels for 40%

profile of v2, /device:TPU:1, one launch (start us, length us, event | category | flops | bytes accessed | tf_op | source)
XLA Modules:
  0.0 223.2 jit_solution(1942997521836734129)
XLA Ops:
  7.2 0.0 copy-start.3
  7.2 0.0 all-gather.2.cloned.1.call-start
  7.2 0.0 copy-start.4
  7.2 1.3 copy-done.4
  8.5 0.0 copy-start.11
  8.5 0.0 copy-start.12
  8.5 0.0 copy-start.10
  8.5 1.7 shard_map.129.w_ref
  10.2 0.0 all-gather.2.cloned.1.call-update
  10.2 0.0 copy-start.1
  10.2 0.0 copy-start.9
  10.3 0.0 copy-done.3
  10.3 0.0 copy-done.11
  10.3 0.0 copy-done.12
  10.3 78.8 %shard_map.130 = (bf16[256,1024]{1,0:T(8,128)(2,1)S(1)}, f32[2048,384]{1,0:T(8,128)}, bf16[2048,384]{1,0:T(8,128)(2,1)S(1)}, bf16[512,256]{1,0:T(8,128)(2,1)S(1)}, bf16[512,256]{1,0:T(8,128)(2,1)S(1)}) custom-call(s32[1,256]{1,0:T(1,128)S(1)} %bitcast.6, s32[1,256]{1,0:T(1,128)S(1)} %bitcast.7, bf16[256,1024]{1,0:T(8,128)(2,1)S(1)} %copy-done.3, ...), custom_call_target="tpu_custom_call" | custom-call | tf_op jit(solution)/shard_map/pallas_call | solution.py:574
  89.1 0.0 copy-start.5
  89.1 0.8 copy-done.5
  89.9 0.0 copy-start.7
  89.9 0.7 copy-done.7
  90.6 0.0 copy-done.10
  90.6 11.3 %shard_map.131.att_ref = bf16[2048,128]{1,0:T(8,128)(2,1)S(1)} custom-call(s32[1,4]{1,0:T(1,128)S(1)} %copy-done.10, bf16[2048,384]{1,0:T(8,128)(2,1)S(1)} %get-tuple-element.12.qkv_ref), custom_call_target="tpu_custom_call" | custom-call | tf_op jit(solution)/shard_map/pallas_call | solution.py:600
  101.9 0.0 all-gather.2.cloned.1.call-done.w_ref
  101.9 0.0 copy-done.1
  101.9 0.0 copy-done.9
  102.0 0.0 copy-start.2
  102.0 1.6 copy-done.2
  103.5 0.0 copy-start.6
  103.6 1.0 copy-done.6
  104.6 0.0 copy-start
  104.6 18.3 %shard_map.132 = (f32[256,1024]{1,0:T(8,128)S(1)}, bf16[8,256,128]{2,1,0:T(8,128)(2,1)S(1)}, bf16[8,256,128]{2,1,0:T(8,128)(2,1)S(1)}) custom-call(bf16[2048,128]{1,0:T(8,128)(2,1)S(1)} %shard_map.131.att_ref, bf16[256,1024]{1,0:T(8,128)(2,1)S(1)} %copy-done.6, bf16[8192,512]{1,0:T(8,128)(2,1)} %all-gather.2.cloned.1.call-done.w_ref, ...), custom_call_target="tpu_custom_call" | custom-call | tf_op jit(solution)/shard_map/pallas_call | solution.py:601
  122.9 0.0 copy-done
  122.9 0.0 copy-start.8
  122.9 19.9 %shard_map.133.dqkv_ref = bf16[2048,384]{1,0:T(8,128)(2,1)S(1)} custom-call(s32[1,4]{1,0:T(1,128)S(1)} %copy-done.10, bf16[2048,384]{1,0:T(8,128)(2,1)S(1)} %get-tuple-element.12.qkv_ref, f32[2048,384]{1,0:T(8,128)S(1)} %copy-done, bf16[2048,128]{1,0:T(8,128)(2,1)S(1)} %bitcast.4), custom_call_target="tpu_custom_call" | custom-call | tf_op jit(solution)/shard_map/pallas_call | solution.py:624
  142.8 0.0 copy-done.8
  142.8 0.0 copy-start.13
  142.8 0.0 copy-start.14
  142.8 70.3 %shard_map.134 = f32[256,1024]{1,0:T(8,128)S(1)} custom-call(bf16[2048,384]{1,0:T(8,128)(2,1)S(1)} %shard_map.133.dqkv_ref, bf16[8,256,128]{2,1,0:T(8,128)(2,1)S(1)} %get-tuple-element.17.dpu_ref, bf16[512,256]{1,0:T(8,128)(2,1)S(1)} %copy-done.8, bf16[512,256]{1,0:T(8,128)(2,1)S(1)} %get-tuple-element.19.wanted_ref, ...), custom_call_target="tpu_custom_call" | custom-call | tf_op jit(solution)/shard_map/pallas_call | solution.py:631
  213.1 0.0 copy-done.13
  213.1 0.0 copy-done.14
  213.1 2.3 %multiply_subtract_fusion = (f32[256,1024]{1,0:T(8,128)}, f32[256,1024]{1,0:T(8,128)}, f32[256,1024]{1,0:T(8,128)}) fusion(bf16[256,1024]{1,0:T(8,128)(2,1)S(1)} %copy-done.3, f32[256,1024]{1,0:T(8,128)S(1)} %shard_map.134, f32[256,1024]{1,0:T(8,128)S(1)} %copy-done.13, f32[256,1024]{1,0:T(8,128)S(1)} %copy-done.14), kind=kLoop, calls=%fused_computation.2 | loop fusion | flops 3670016 | bytes 6815744 | tf_op jit(solution)/shard_map/sub | solution.py:544
  215.4 1.0 copy.15
Async XLA Ops:
  7.2 3.1 %copy-start.3 = (bf16[256,1024]{1,0:T(8,128)(2,1)S(1)}, bf16[256,1024]{1,0:T(8,128)(2,1)}, u32[]{:S(2)}) copy-start(bf16[256,1024]{1,0:T(8,128)(2,1)} %table_ref.1) | copy-start | bytes 1572868
  7.2 94.8 %all-gather.2.cloned.1.call-start = ((), (), s32[]{:S(2)}) async-start(), calls=%async_computation | async-start | bytes 9437184 | tf_op jit(solution)/shard_map/all_gather | solution.py:572
  7.2 1.3 copy-start.4
  8.5 1.8 copy-start.11
  8.5 1.8 copy-start.12
  8.5 82.1 %copy-start.10 = (s32[1,4]{1,0:T(1,128)S(1)}, s32[1,4]{1,0:T(1,128)}, u32[]{:S(2)}) copy-start(s32[1,4]{1,0:T(1,128)} %len_ref.3) | copy-start | bytes 52
  10.2 91.7 %copy-start.1 = (bf16[256,1024]{1,0:T(8,128)(2,1)S(1)}, bf16[256,1024]{1,0:T(8,128)(2,1)}, u32[]{:S(2)}) copy-start(bf16[256,1024]{1,0:T(8,128)(2,1)} %up_ref.3) | copy-start | bytes 1572868
  10.2 91.7 %copy-start.9 = (f32[1024]{0:T(1024)S(1)}, f32[1024]{0:T(1024)}, u32[]{:S(2)}) copy-start(f32[1024]{0:T(1024)} %param.18) | copy-start | bytes 12292
  89.1 0.8 copy-start.5
  89.9 0.7 copy-start.7
  102.0 1.6 copy-start.2
  103.5 1.0 copy-start.6
  104.6 18.3 %copy-start = (f32[2048,384]{1,0:T(8,128)S(1)}, f32[2048,384]{1,0:T(8,128)}, u32[]{:S(2)}) copy-start(f32[2048,384]{1,0:T(8,128)} %get-tuple-element.15.pre_ref) | copy-start | bytes 9437188
  122.9 19.9 %copy-start.8 = (bf16[512,256]{1,0:T(8,128)(2,1)S(1)}, bf16[512,256]{1,0:T(8,128)(2,1)}, u32[]{:S(2)}) copy-start(bf16[512,256]{1,0:T(8,128)(2,1)} %copy-done.7) | copy-start | bytes 786436
  142.8 70.3 %copy-start.13 = (f32[256,1024]{1,0:T(8,128)S(1)}, f32[256,1024]{1,0:T(8,128)}, u32[]{:S(2)}) copy-start(f32[256,1024]{1,0:T(8,128)} %param.11) | copy-start | bytes 3145732
  142.8 70.3 %copy-start.14 = (f32[256,1024]{1,0:T(8,128)S(1)}, f32[256,1024]{1,0:T(8,128)}, u32[]{:S(2)}) copy-start(f32[256,1024]{1,0:T(8,128)} %param.12) | copy-start | bytes 3145732
Sparse Core Ops, SparseCore 0:
  10.4 66.2 all-gather.1

commit v3 on v2

--- a/solution.py
+++ b/solution.py
@@ -21,7 +21,8 @@
 
 BF = jnp.bfloat16
 F32 = jnp.float32
-BLOCK = 256
+FWD_Q, FWD_K = 512, 256
+BACK_Q, BACK_K = 512, 256
 NT = (((1,), (1,)), ((), ()))
 TN = (((0,), (0,)), ((), ()))
 
@@ -73,27 +74,28 @@
     tokens = qkv_ref.shape[0]
     ends = ends_of(len_ref)
 
-    @pl.loop(0, tokens // BLOCK)
+    @pl.loop(0, tokens // FWD_Q)
     def _(qb):
-        q0 = qb * BLOCK
-        qs = by_head(qkv_ref[pl.ds(q0, BLOCK), 0:PAIR]) * jnp.asarray(SCALE, BF)
-        row = lax.broadcasted_iota(jnp.int32, (2 * BLOCK, 1), 0)
-        i = q0 + jnp.where(row >= BLOCK, row - BLOCK, row)
+        q0 = qb * FWD_Q
+        qs = by_head(qkv_ref[pl.ds(q0, FWD_Q), 0:PAIR]) * jnp.asarray(0.5 * SCALE, BF)
+        row = lax.broadcasted_iota(jnp.int32, (2 * FWD_Q, 1), 0)
+        i = q0 + jnp.where(row >= FWD_Q, row - FWD_Q, row)
         start_i = start_at(i, ends)
 
         def step(kb, acc):
-            k0 = kb * BLOCK
-            k = qkv_ref[pl.ds(k0, BLOCK), PAIR : 2 * PAIR]
-            v = qkv_ref[pl.ds(k0, BLOCK), 2 * PAIR : 3 * PAIR]
-            s = mm(qs, k, NT)
-            j = k0 + lax.broadcasted_iota(jnp.int32, s.shape, 1)
+            k0 = kb * FWD_K
+            k = qkv_ref[pl.ds(k0, FWD_K), PAIR : 2 * PAIR]
+            v = qkv_ref[pl.ds(k0, FWD_K), 2 * PAIR : 3 * PAIR]
+            h = mm(qs, k, NT)
+            j = k0 + lax.broadcasted_iota(jnp.int32, h.shape, 1)
             visible = (j >= start_i) & (j <= i)
-            w = jnp.where(visible, s * sigmoid(s), 0.0).astype(BF)
+            w = jnp.where(visible, h + h * jnp.tanh(h), 0.0).astype(BF)
             return acc + mm(w, v)
 
-        first = lax.div(start_at(q0, ends), BLOCK)
-        acc = lax.fori_loop(first, qb + 1, step, jnp.zeros((2 * BLOCK, PAIR), F32))
-        out_ref[pl.ds(q0, BLOCK), :] = merge_heads(acc).astype(BF)
+        first = lax.div(start_at(q0, ends), FWD_K)
+        last = lax.div(q0 + FWD_Q - 1, FWD_K)
+        acc = lax.fori_loop(first, last + 1, step, jnp.zeros((2 * FWD_Q, PAIR), F32))
+        out_ref[pl.ds(q0, FWD_Q), :] = merge_heads(acc).astype(BF)
 
 
 def attend_back_kernel(len_ref, qkv_ref, pre_ref, do_ref, out_ref, dq_ref):
@@ -105,48 +107,55 @@
         slope = silu_pair(pre_ref[rows, part * PAIR : (part + 1) * PAIR])[1]
         out_ref[rows, part * PAIR : (part + 1) * PAIR] = (d_part.astype(BF).astype(F32) * slope).astype(BF)
 
-    @pl.loop(0, tokens // BLOCK)
+    @pl.loop(0, tokens // BACK_K)
     def _(kb):
-        k0 = kb * BLOCK
-        rows = pl.ds(k0, BLOCK)
+        k0 = kb * BACK_K
+        rows = pl.ds(k0, BACK_K)
         k = qkv_ref[rows, PAIR : 2 * PAIR]
-        v = qkv_ref[rows, 2 * PAIR : 3 * PAIR]
+        v = qkv_ref[rows, 2 * PAIR : 3 * PAIR] * jnp.asarray(0.5, BF)
 
         def step(qb, carry):
             dk, dv = carry
-            q0 = qb * BLOCK
-            qs = by_head(qkv_ref[pl.ds(q0, BLOCK), 0:PAIR]) * jnp.asarray(SCALE, BF)
-            dos = by_head(do_ref[pl.ds(q0, BLOCK), :])
-            s = mm(k, qs, NT)
+            q0 = qb * BACK_Q
+            qs = by_head(qkv_ref[pl.ds(q0, BACK_Q), 0:PAIR]) * jnp.asarray(0.5 * SCALE, BF)
+            dos = by_head(do_ref[pl.ds(q0, BACK_Q), :])
+            h = mm(k, qs, NT)
             dw = mm(v, dos, NT)
-            act, slope = silu_pair(s)
-            col = lax.broadcasted_iota(jnp.int32, (1, 2 * BLOCK), 1)
-            i = q0 + jnp.where(col >= BLOCK, col - BLOCK, col)
+            rise = 1.0 + jnp.tanh(h)
+            act = h * rise
+            slope = rise * ((1.0 + 2.0 * h) - act)
+            col = lax.broadcasted_iota(jnp.int32, (1, 2 * BACK_Q), 1)
+            i = q0 + jnp.where(col >= BACK_Q, col - BACK_Q, col)
             start_i = start_at(i, ends)
-            j = k0 + lax.broadcasted_iota(jnp.int32, s.shape, 0)
+            j = k0 + lax.broadcasted_iota(jnp.int32, h.shape, 0)
             visible = (j >= start_i) & (j <= i)
             w = jnp.where(visible, act, 0.0).astype(BF)
             ds = jnp.where(visible, dw * slope, 0.0).astype(BF)
             dq = mm(ds, k, TN)
-            dq_ref[pl.ds(q0, BLOCK), :] += merge_heads(dq)
+            dq_ref[pl.ds(q0, BACK_Q), :] += merge_heads(dq)
             return dk + mm(ds, qs), dv + mm(w, dos)
 
-        last = lax.div(stop_at(k0 + BLOCK - 1, ends, tokens) - 1, BLOCK)
-        zero = jnp.zeros((BLOCK, PAIR), F32)
-        dk, dv = lax.fori_loop(kb, last + 1, step, (zero, zero))
+        first = lax.div(k0, BACK_Q)
+        last = lax.div(stop_at(k0 + BACK_K - 1, ends, tokens) - 1, BACK_Q)
+        zero = jnp.zeros((BACK_K, PAIR), F32)
+        dk, dv = lax.fori_loop(first, last + 1, step, (zero, zero))
+        finish_part(rows, 1, dk * 2.0)
+        finish_part(rows, 2, dv)
+
+    @pl.loop(0, tokens // BACK_K)
+    def _(qb):
+        rows = pl.ds(qb * BACK_K, BACK_K)
         finish_part(rows, 0, dq_ref[rows, :] * SCALE)
-        finish_part(rows, 1, dk)
-        finish_part(rows, 2, dv)
-
-
-def shuffle_kernel(w_ref, out_ref):
-    size = w_ref.shape[1]
+
+
+def by_parts(w):
+    size = w.shape[1]
     row = lax.broadcasted_iota(jnp.int32, (size, size), 0)
     col = lax.broadcasted_iota(jnp.int32, (size, size), 1)
     lane = lax.rem(col, PAIR)
     source = lax.div(lane, DH) * (4 * DH) + lax.div(col, PAIR) * DH + lax.rem(lane, DH)
     move = jnp.where(row == source, 1.0, 0.0).astype(BF)
-    out_ref[...] = mm(w_ref[...], move).astype(BF)
+    return mm(w, move).astype(BF)
 
 
 def group_peers(k, groups):
@@ -199,15 +208,17 @@
 
 
 def fetch_kernel(
-    groups, seq, owner_ref, index_ref, table_ref, w_ref,
-    emb_ref, pre_ref, qkv_ref, wanted_ref, place_ref,
-    ask_out, ask_in, row_out, row_in, ring, ask_s, ask_r, row_s, row_r, ring_s, ring_r,
+    groups, seq, names_ref, table_ref, w_ref,
+    emb_ref, pre_ref, qkv_ref, wanted_ref, place_ref, w_all,
+    w_own, table, load_s, w_s, w_r, ask_out, ask_in, row_out, row_in, ring, ask_s, ask_r, row_s, row_r, ring_s, ring_r,
 ):
     chunks, slots, cut = row_out.shape
-    rows = owner_ref.shape[1]
+    rows = names_ref.shape[1]
     cap = slots // groups
-    table_rows = table_ref.shape[0]
+    table_rows, width = table_ref.shape
     wide = 3 * PAIR
+    parts = w_s.shape[0]
+    deep = width // parts
     g, s = lax.axis_index("group"), lax.axis_index("seq")
     chips = seq // 2
     x, core = lax.div(s, 2), lax.rem(s, 2)
@@ -217,11 +228,25 @@
     across = lax.rem(x + 2, chips) * 2 + core
     sib = s + flip
 
+    load_w = pltpu.make_async_copy(w_ref, w_own, load_s.at[0])
+    load_table = pltpu.make_async_copy(table_ref, table, load_s.at[1])
+    load_w.start()
+    load_table.start()
     barrier, greeted = greet(groups, [sib, right, left], seq)
-    place_ref[...] = slot_places(owner_ref[...], slots, groups)
-    index = jnp.broadcast_to((index_ref[...] + 1).astype(F32), (PAIR, rows)).astype(BF)
+    place_ref[...] = slot_places(names_ref[0:1], slots, groups)
+    index = jnp.broadcast_to((names_ref[1:2] + 1).astype(F32), (PAIR, rows)).astype(BF)
     ask_out[...] = mm(place_ref[...], index, NT).astype(BF)
+    load_w.wait()
+    for j in range(parts):
+        w_own[j * deep : (j + 1) * deep] = by_parts(w_own[j * deep : (j + 1) * deep])
+    keep_w = pltpu.make_async_copy(w_own, w_all.at[pl.ds(pl.multiple_of(s * width, width), width)], load_s.at[2])
+    keep_w.start()
     pl.semaphore_wait(barrier, greeted)
+
+    def w_hop(j, op, block, to, low=0, size=deep):
+        at = pl.ds(pl.multiple_of(block * width + j * deep + low, size), size)
+        src = w_own.at[pl.ds(j * deep, deep)] if op < 3 else w_all.at[at]
+        return send(src, w_all.at[at], w_s.at[j, op], w_r.at[j, op], seq=to)
 
     mine = pl.ds(pl.multiple_of(g * cap, cap), cap)
 
@@ -242,6 +267,10 @@
     def _(k):
         ask(k).start()
 
+    for j in range(parts):
+        w_hop(j, 1, s, right).start()
+        w_hop(j, 2, s, left).start()
+        w_hop(j, 0, s, sib).start()
     ask_in[mine] = ask_out[mine]
 
     @pl.loop(1, groups)
@@ -253,11 +282,14 @@
         lane = lax.broadcasted_iota(jnp.int32, wanted.shape, 1) + (part * PAIR + 1)
         wanted_ref[:, part * PAIR : (part + 1) * PAIR] = jnp.where(wanted == lane, 1.0, 0.0).astype(BF)
 
+    load_table.wait()
     for c in range(chunks):
-        row_out[c] = mm(wanted_ref[...], table_ref[:, c * cut : (c + 1) * cut]).astype(BF)
+        row_out[c] = mm(wanted_ref[...], table[:, c * cut : (c + 1) * cut]).astype(BF)
 
         @pl.loop(1, groups)
         def _(k):
+            if c > 0:
+                give(c - 1, k).wait_send()
             give(c, k).start()
 
         row_in[c, mine] = row_out[c, mine]
@@ -270,18 +302,19 @@
 
     def project(c, block):
         at = pl.ds(pl.multiple_of(block * rows, rows), rows)
-        val = mm(ring[c, block], w_ref[c * cut : (c + 1) * cut, :wide])
+        val = mm(ring[c, block], w_own[c * cut : (c + 1) * cut, :wide])
         if c > 0:
             val = val + pre_ref[at]
         pre_ref[at] = val
         if c == chunks - 1:
             qkv_ref[at] = silu_pair(val)[0].astype(BF)
 
-    for c in range(chunks):
-
+    def gathered(c):
         @pl.loop(1, groups)
         def _(k):
-            give(c, k).wait()
+            give(c, k).wait_recv()
+            if c == chunks - 1:
+                give(c, k).wait_send()
 
         block = mm(place_ref[...], row_in[c], TN).astype(BF)
         emb_ref[:, c * cut : (c + 1) * cut] = block
@@ -290,6 +323,8 @@
         hop(c, 2, s, left).start()
         hop(c, 0, s, sib).start()
         project(c, s)
+
+    def first_hop(c):
         hop(c, 1, left, right).wait_recv()
         hop(c, 3, left, right, 0, half).start()
         hop(c, 4, left, sib).start()
@@ -300,11 +335,15 @@
         project(c, right)
         hop(c, 0, sib, sib).wait_recv()
         project(c, sib)
+
+    def second_hop(c):
         hop(c, 3, across, right, 0, half).wait_recv()
         hop(c, 7, across, sib, 0, half).start()
         hop(c, 5, across, left, half, half).wait_recv()
         hop(c, 8, across, sib, half, half).start()
         project(c, across)
+
+    def from_sibling(c):
         hop(c, 4, left + flip, sib).wait_recv()
         project(c, left + flip)
         hop(c, 6, right + flip, sib).wait_recv()
@@ -313,6 +352,45 @@
         hop(c, 8, across + flip, sib, half, half).wait_recv()
         project(c, across + flip)
 
+    for c in range(chunks):
+        gathered(c)
+        if c == 0:
+            for j in range(parts):
+                w_hop(j, 1, left, right).wait_recv()
+                w_hop(j, 3, left, right, 0, deep // 2).start()
+                w_hop(j, 4, left, sib).start()
+                w_hop(j, 2, right, left).wait_recv()
+                w_hop(j, 5, right, left, deep // 2, deep // 2).start()
+                w_hop(j, 6, right, sib).start()
+        if c > 0:
+            second_hop(c - 1)
+        first_hop(c)
+        if c > 0:
+            from_sibling(c - 1)
+    second_hop(chunks - 1)
+    from_sibling(chunks - 1)
+
+    for j in range(parts):
+        w_hop(j, 3, across, right, 0, deep // 2).wait_recv()
+        w_hop(j, 7, across, sib, 0, deep // 2).start()
+        w_hop(j, 5, across, left, deep // 2, deep // 2).wait_recv()
+        w_hop(j, 8, across, sib, deep // 2, deep // 2).start()
+    for j in range(parts):
+        w_hop(j, 0, sib, sib).wait_recv()
+        w_hop(j, 4, left + flip, sib).wait_recv()
+        w_hop(j, 6, right + flip, sib).wait_recv()
+        w_hop(j, 7, across + flip, sib, 0, deep // 2).wait_recv()
+        w_hop(j, 8, across + flip, sib, deep // 2, deep // 2).wait_recv()
+        w_hop(j, 0, s, sib).wait_send()
+        w_hop(j, 1, s, right).wait_send()
+        w_hop(j, 2, s, left).wait_send()
+        w_hop(j, 3, left, right, 0, deep // 2).wait_send()
+        w_hop(j, 4, left, sib).wait_send()
+        w_hop(j, 5, right, left, deep // 2, deep // 2).wait_send()
+        w_hop(j, 6, right, sib).wait_send()
+        w_hop(j, 7, across, sib, 0, deep // 2).wait_send()
+        w_hop(j, 8, across, sib, deep // 2, deep // 2).wait_send()
+    keep_w.wait()
     for c in range(chunks):
         hop(c, 1, s, right).wait_send()
         hop(c, 2, s, left).wait_send()
@@ -328,7 +406,7 @@
 def middle_kernel(
     seq, att_ref, emb_ref, w_ref, wo_ref, gain_ref, up_ref,
     layer_ref, dheads_ref, dpu_ref,
-    wu, att_in, datt_out, datt_in, d_mixed, pre_u, w_s, att_s, att_r, datt_s, datt_r,
+    wu, wo, mixed, att_in, datt_out, datt_in, d_mixed, pre_u, w_s, wo_s, att_s, att_r, datt_s, datt_r,
 ):
     rows, width = emb_ref.shape
     s = lax.axis_index("seq")
@@ -339,61 +417,72 @@
             w_ref.at[pl.ds(b * width, width), 3 * PAIR : 4 * PAIR], wu.at[b], w_s.at[b]
         )
 
+    load_wo = pltpu.make_async_copy(wo_ref, wo, wo_s)
+    load_wo.start()
     for b in range(seq):
         load(b).start()
     barrier, greeted = greet(1, [seq_peer(k, seq) for k in range(1, seq)], seq)
     pl.semaphore_wait(barrier, greeted)
 
-    def hand(k):
+    half = rows // HALVES
+
+    def hand(h, k):
         to = seq_peer(k, seq)
         return send(
-            att_ref.at[pl.ds(pl.multiple_of(to * rows, rows), rows)], att_in.at[s], att_s.at[k], att_r.at[k], seq=to
+            att_ref.at[pl.ds(pl.multiple_of(to * rows + h * half, half), half)],
+            att_in.at[s, h * half : (h + 1) * half], att_s.at[h, k], att_r.at[h, k], seq=to,
         )
 
-    def back(k):
+    def back(h, k):
         to = seq_peer(k, seq)
-        return send(datt_out.at[to], datt_in.at[s], datt_s.at[k], datt_r.at[k], seq=to)
-
-    for k in order:
-        hand(k).start()
+        part = slice(h * half, (h + 1) * half)
+        return send(datt_out.at[to, part], datt_in.at[s, part], datt_s.at[h, k], datt_r.at[h, k], seq=to)
+
+    for h in range(HALVES):
+        for k in order:
+            hand(h, k).start()
     att_in[s] = att_ref[pl.ds(pl.multiple_of(s * rows, rows), rows)]
-    d_mixed[...] = mm(up_ref[...], wo_ref[...], NT)
+    load_wo.wait()
+    d_mixed[...] = mm(up_ref[...], wo[...], NT)
     emb = emb_ref[...]
     for b in range(seq):
         load(b).wait()
         pre_u[:, b * PAIR : (b + 1) * PAIR] = mm(emb, wu[b])
-    for k in order:
-        hand(k).wait()
-
-    att = jnp.concatenate([att_in[b] for b in range(seq)], axis=1).astype(F32)
-    center = att - jnp.mean(att, axis=-1, keepdims=True)
-    spread = jnp.mean(center * center, axis=-1, keepdims=True)
-    r = lax.rsqrt(spread + norm_eps)
-    xhat = center * r
     gain = gain_ref[...]
-    normed = xhat * gain
-    act_u, slope_u = silu_pair(pre_u[...])
-    u = act_u.astype(BF).astype(F32)
-    d_mix = d_mixed[...]
-    gx = d_mix * u * gain
-    datt = r * (
-        gx
-        - jnp.mean(gx, axis=-1, keepdims=True)
-        - xhat * jnp.mean(gx * xhat, axis=-1, keepdims=True)
-    )
-    datt = datt.astype(BF)
-    for b in range(seq):
-        datt_out[b] = datt[:, b * PAIR : (b + 1) * PAIR]
-    for k in order:
-        back(k).start()
+    for h in range(HALVES):
+        part = slice(h * half, (h + 1) * half)
+        for k in order:
+            hand(h, k).wait_recv()
+        att = jnp.concatenate([att_in[b, part] for b in range(seq)], axis=1).astype(F32)
+        center = att - jnp.mean(att, axis=-1, keepdims=True)
+        spread = jnp.mean(center * center, axis=-1, keepdims=True)
+        r = lax.rsqrt(spread + norm_eps)
+        xhat = center * r
+        act_u, slope_u = silu_pair(pre_u[part])
+        u = act_u.astype(BF).astype(F32)
+        d_mix = d_mixed[part]
+        gx = d_mix * u * gain
+        datt = r * (
+            gx
+            - jnp.mean(gx, axis=-1, keepdims=True)
+            - xhat * jnp.mean(gx * xhat, axis=-1, keepdims=True)
+        )
+        datt = datt.astype(BF)
+        for b in range(seq):
+            datt_out[b, part] = datt[:, b * PAIR : (b + 1) * PAIR]
+        for k in order:
+            back(h, k).start()
+        normed = xhat * gain
+        dpu = ((d_mix * normed).astype(BF).astype(F32) * slope_u).astype(BF)
+        for b in range(seq):
+            dpu_ref[b, part] = dpu[:, b * PAIR : (b + 1) * PAIR]
+        mixed[part] = (normed * u).astype(BF)
     datt_in[s] = datt_out[s]
-    dpu = ((d_mix * normed).astype(BF).astype(F32) * slope_u).astype(BF)
-    for b in range(seq):
-        dpu_ref[b] = dpu[:, b * PAIR : (b + 1) * PAIR]
-    mixed = (normed * u).astype(BF)
-    layer_ref[...] = emb.astype(F32) + mm(mixed, wo_ref[...])
-    for k in order:
-        back(k).wait()
+    layer_ref[...] = emb.astype(F32) + mm(mixed[...], wo[...])
+    for h in range(HALVES):
+        for k in order:
+            hand(h, k).wait_send()
+            back(h, k).wait()
     dheads_ref[...] = datt_in[...]
 
 
@@ -442,9 +531,18 @@
         to = seq_peer(k, seq)
         return send(part.at[c, to], part_in.at[c, s], part_s.at[c, k], part_r.at[c, k], seq=to)
 
-    def copy_share(c, k):
-        to = seq_peer(k, seq)
-        return send(share.at[c], share_in.at[c, s], share_s.at[c, k], share_r.at[c, k], seq=to)
+    x, core = lax.div(s, 2), lax.rem(s, 2)
+    sib = s + 1 - 2 * core
+    chips = seq // 2
+
+    def copy_share(c, dx):
+        to = sib if dx == 0 else lax.rem(x + dx, chips) * 2 + core
+        return send(share.at[c], share_in.at[c, s], share_s.at[c, dx], share_r.at[c, dx], seq=to)
+
+    def pass_share(c, dx):
+        block = lax.rem(x + chips - dx, chips) * 2 + core
+        view = share_in.at[c, block]
+        return send(view, view, share_s.at[c, chips + dx], share_r.at[c, chips + dx], seq=sib)
 
     for k in order:
         hand(k).start()
@@ -463,6 +561,8 @@
 
         @pl.loop(1, groups)
         def _(k):
+            if c > 0:
+                give(c - 1, k).wait_send()
             give(c, k).start()
 
         row_in[c, mine] = row_out[c, mine]
@@ -471,7 +571,9 @@
 
         @pl.loop(1, groups)
         def _(k):
-            give(c, k).wait()
+            give(c, k).wait_recv()
+            if c == chunks - 1:
+                give(c, k).wait_send()
 
         sums = mm(wanted_ref[...], row_in[c], TN)
         for b in range(seq):
@@ -484,13 +586,17 @@
             spread(c, k).wait_recv()
             total = total + part_in[c, lax.rem(s + seq - k, seq)].astype(F32)
         share[c] = total
-        for k in order:
-            copy_share(c, k).start()
+        for dx in [2, 1, 3, 0]:
+            copy_share(c, dx).start()
         share_in[c, s] = total
 
     for c in range(chunks):
-        for k in order:
-            copy_share(c, k).wait()
+        for dx in [1, 3, 2]:
+            copy_share(c, dx).wait()
+            pass_share(c, dx).start()
+        copy_share(c, 0).wait()
+        for dx in [1, 3, 2]:
+            pass_share(c, dx).wait()
         for b in range(seq):
             grad_ref[b * own : (b + 1) * own, c * cut : (c + 1) * cut] = share_in[c, b]
         for k in order:
@@ -515,12 +621,12 @@
     )
 
 
-def remote_call(kernel, ident, out_shape, specs, scratch, limit=48):
+def remote_call(kernel, ident, out_shape, specs, scratch, out_specs=None, limit=48):
     return pl.pallas_call(
         kernel,
         out_shape=out_shape,
         in_specs=specs,
-        out_specs=jax.tree.map(lambda _: VM, out_shape),
+        out_specs=out_specs or jax.tree.map(lambda _: VM, out_shape),
         scratch_shapes=list(scratch),
         compiler_params=pltpu.CompilerParams(
             collective_id=ident, has_side_effects=True, vmem_limit_bytes=limit * MIB
@@ -529,7 +635,10 @@
 
 
 ANY = pl.BlockSpec(memory_space=pl.ANY)
+HBM = pl.BlockSpec(memory_space=pltpu.HBM)
 CHUNKS = 2
+W_PARTS = 2
+HALVES = 2
 DMA = pltpu.SemaphoreType.DMA
 
 
@@ -568,10 +677,7 @@
 
     cut = width // CHUNKS
 
-    w_own = local_call(shuffle_kernel, sds(proj_weight.shape, BF), [VM])(proj_weight)
-    w_all = lax.all_gather(w_own, "seq", axis=0, tiled=True)
-
-    embedded, pre, qkv, wanted, place = remote_call(
+    embedded, pre, qkv, wanted, place, w_all = remote_call(
         functools.partial(fetch_kernel, groups, seq),
         1,
         (
@@ -580,9 +686,15 @@
             sds((tokens, 3 * PAIR), BF),
             sds((slots, table_rows), BF),
             sds((slots, tok_rows), BF),
+            sds((seq * width, 4 * PAIR), BF),
         ),
-        [VM] * 4,
+        [VM, HBM, HBM],
         [
+            pltpu.VMEM((width, 4 * PAIR), BF),
+            pltpu.VMEM((table_rows, width), BF),
+            DMA((3,)),
+            DMA((W_PARTS, 9)),
+            DMA((W_PARTS, 9)),
             pltpu.VMEM((slots, PAIR), BF),
             pltpu.VMEM((slots, PAIR), BF),
             pltpu.VMEM((CHUNKS, slots, cut), BF),
@@ -595,7 +707,8 @@
             DMA((CHUNKS, 9)),
             DMA((CHUNKS, 9)),
         ],
-    )(row_owner.reshape(1, -1), row_index.reshape(1, -1), embed_table, w_own)
+        (VM,) * 5 + (HBM,),
+    )(jnp.stack([row_owner[:, 0], row_index]), embed_table, proj_weight)
 
     att_heads = local_call(attend_kernel, sds((tokens, PAIR), BF), [SM, VM])(lengths, qkv)
     layer_out, d_heads, d_pre_u = remote_call(
@@ -606,19 +719,22 @@
             sds((seq, tok_rows, PAIR), BF),
             sds((seq, tok_rows, PAIR), BF),
         ),
-        [VM, VM, ANY, VM, VM, VM],
+        [VM, VM, ANY, ANY, VM, VM],
         [
             pltpu.VMEM((seq, width, PAIR), BF),
+            pltpu.VMEM((width, width), BF),
+            pltpu.VMEM((tok_rows, width), BF),
             pltpu.VMEM((seq, tok_rows, PAIR), BF),
             pltpu.VMEM((seq, tok_rows, PAIR), BF),
             pltpu.VMEM((seq, tok_rows, PAIR), BF),
             pltpu.VMEM((tok_rows, width), F32),
             pltpu.VMEM((tok_rows, width), F32),
             DMA((seq,)),
-            DMA((seq,)),
-            DMA((seq,)),
-            DMA((seq,)),
-            DMA((seq,)),
+            DMA,
+            DMA((HALVES, seq)),
+            DMA((HALVES, seq)),
+            DMA((HALVES, seq)),
+            DMA((HALVES, seq)),
         ],
     )(att_heads, embedded, w_all, out_weight, norm_gain.reshape(1, -1), upstream)
     d_pre_heads = local_call(

time: 224 us -> 200 us (0.89)
  between operations: 14.2 us -> 0.79 us
  Pallas kernels: 200 us -> 192 us
  local copies, waits for them, and re-layouts: 6.4 us -> 3.92 us
    pallas_call x1, Pallas kernels: 78.8 us -> 75 us  [body(): remote_call(functools.partial(fetch_kernel, groups, seq), 1, (sds((tok_ro...]
    unnamed x31 -> x21, local copies, waits for them, and re-layouts: 6.4 us -> 3.92 us
    pallas_call x1, Pallas kernels: 70.3 us -> 72.7 us  [body(): remote_call(functools.partial(back_kernel, groups, seq), 3, sds((table_ro...]
    pallas_call x1, Pallas kernels: 11.3 us -> 8.92 us  [body(): local_call(attend_kernel, sds((tokens, PAIR), BF), [SM, VM])(lengths, qkv)]
  transfers between devices with their start and end apart: 1 -> 0, of which waited for: 0 -> 0; matrix products, arithmetic and copies ran while one was open for 0% -> 0% of each run, Pallas kernels for 40% -> 0%
where the time goes in v3:
time: 200 us; the launch traced here: 199 us
  Pallas kernels  192 us (96%)
  local copies, waits for them, and re-layouts  3.92 us (2%)
  other arithmetic  3.05 us (2%)
    pallas_call x1, Pallas kernels, body(): remote_call(functools.partial(fetch_kernel, groups, seq), 1, (sds((tok_ro...  75 us
    pallas_call x1, Pallas kernels, body(): remote_call(functools.partial(back_kernel, groups, seq), 3, sds((table_ro...  72.7 us
    pallas_call x1, Pallas kernels, body(): local_call(attend_back_kernel, sds((tokens, 3 * PAIR), BF), [SM, VM, VM,...  17.8 us
    pallas_call x1, Pallas kernels, body(): remote_call(functools.partial(middle_kernel, seq), 2, (sds((tok_rows, wid...  17.3 us
    pallas_call x1, Pallas kernels, body(): local_call(attend_kernel, sds((tokens, PAIR), BF), [SM, VM])(lengths, qkv)  8.92 us

profile of v3, /device:TPU:1, one launch (start us, length us, event | category | flops | bytes accessed | tf_op | source)
XLA Modules:
  0.0 199.4 jit_solution(15732046372829572335)
XLA Ops:
  0.6 0.0 copy-start.1
  0.6 0.0 copy-start.2
  0.7 0.9 pad_add_fusion.names_ref
  1.5 0.0 copy-start.3
  1.5 1.0 copy-done.3
  2.5 0.0 copy-start.5
  2.6 1.2 copy-done.5
  3.8 0.0 copy-start.6
  3.8 75.0 %shard_map.129 = (bf16[256,1024]{1,0:T(8,128)(2,1)S(1)}, f32[2048,384]{1,0:T(8,128)}, bf16[2048,384]{1,0:T(8,128)(2,1)S(1)}, bf16[512,256]{1,0:T(8,128)(2,1)S(1)...) custom-call(s32[2,256]{1,0:T(2,128)S(1)} %pad_add_fusion.names_ref, bf16[256,1024]{1,0:T(8,128)(2,1)S(1)} %copy-done.3, ...), custom_call_target="tpu_custom_call" | custom-call | tf_op jit(solution)/shard_map/pallas_call | solution.py:680
  78.7 0.0 copy-start.7
  78.8 0.6 copy-done.7
  79.4 8.9 %shard_map.130.att_ref = bf16[2048,128]{1,0:T(8,128)(2,1)S(1)} custom-call(s32[1,4]{1,0:T(1,128)S(1)} %copy-done.7, bf16[2048,384]{1,0:T(8,128)(2,1)S(1)} %get-tuple-element.13.qkv_ref), custom_call_target="tpu_custom_call" | custom-call | tf_op jit(solution)/shard_map/pallas_call | solution.py:713
  88.3 0.0 copy-done.1
  88.3 0.0 copy-done.2
  88.4 0.0 copy-done.6
  88.4 0.0 copy-start
  88.4 17.3 %shard_map.131 = (f32[256,1024]{1,0:T(8,128)S(1)}, bf16[8,256,128]{2,1,0:T(8,128)(2,1)S(1)}, bf16[8,256,128]{2,1,0:T(8,128)(2,1)S(1)}) custom-call(bf16[2048,128]{1,0:T(8,128)(2,1)S(1)} %shard_map.130.att_ref, bf16[256,1024]{1,0:T(8,128)(2,1)S(1)} %get-tuple-element.14.emb_ref, bf16[8192,512]{1,0:T(8,128)(2,1)} %get-tuple-element.15.w_ref, ...), custom_call_target="tpu_custom_call" | custom-call | tf_op jit(solution)/shard_map/pallas_call | solution.py:714
  105.7 0.0 copy-done
  105.7 17.8 %shard_map.132.dqkv_ref = bf16[2048,384]{1,0:T(8,128)(2,1)S(1)} custom-call(s32[1,4]{1,0:T(1,128)S(1)} %copy-done.7, bf16[2048,384]{1,0:T(8,128)(2,1)S(1)} %get-tuple-element.13.qkv_ref, f32[2048,384]{1,0:T(8,128)S(1)} %copy-done, bf16[2048,128]{1,0:T(8,128)(2,1)S(1)} %bitcast.4), custom_call_target="tpu_custom_call" | custom-call | tf_op jit(solution)/shard_map/pallas_call | solution.py:740
  123.5 0.0 copy-start.4
  123.5 0.0 copy-start.8
  123.5 0.0 copy-start.9
  123.5 72.7 %shard_map.133 = f32[256,1024]{1,0:T(8,128)S(1)} custom-call(bf16[2048,384]{1,0:T(8,128)(2,1)S(1)} %shard_map.132.dqkv_ref, bf16[8,256,128]{2,1,0:T(8,128)(2,1)S(1)} %get-tuple-element.19.dpu_ref, bf16[512,256]{1,0:T(8,128)(2,1)S(1)} %get-tuple-element.20.place_ref, bf16[512,256]{1,0:T(8,128)(2,1)S(1)} %get-tuple-element.21.wanted_ref, ...), custom_call_target="tpu_custom_call" | custom-call | tf_op jit(solution)/shard_map/pallas_call | solution.py:747
  196.2 0.0 copy-done.4
  196.2 0.0 copy-done.8
  196.2 0.0 copy-done.9
  196.2 2.2 %multiply_subtract_fusion = (f32[256,1024]{1,0:T(8,128)}, f32[256,1024]{1,0:T(8,128)}, f32[256,1024]{1,0:T(8,128)}) fusion(bf16[256,1024]{1,0:T(8,128)(2,1)S(1)} %copy-done.4, f32[256,1024]{1,0:T(8,128)S(1)} %shard_map.133, f32[256,1024]{1,0:T(8,128)S(1)} %copy-done.8, f32[256,1024]{1,0:T(8,128)S(1)} %copy-done.9), kind=kLoop, calls=%fused_computation.2 | loop fusion | flops 3670016 | bytes 6815744 | tf_op jit(solution)/shard_map/sub | solution.py:653
  198.4 1.0 copy.15
Async XLA Ops:
  0.6 87.7 %copy-start.1 = (bf16[256,1024]{1,0:T(8,128)(2,1)S(1)}, bf16[256,1024]{1,0:T(8,128)(2,1)}, u32[]{:S(2)}) copy-start(bf16[256,1024]{1,0:T(8,128)(2,1)} %up_ref.3) | copy-start | bytes 1572868
  0.6 87.7 %copy-start.2 = (bf16[1024,1024]{1,0:T(8,128)(2,1)S(1)}, bf16[1024,1024]{1,0:T(8,128)(2,1)}, u32[]{:S(2)}) copy-start(bf16[1024,1024]{1,0:T(8,128)(2,1)} %wo_ref.1) | copy-start | bytes 6291460
  1.5 1.0 copy-start.3
  2.5 1.2 copy-start.5
  3.8 84.6 %copy-start.6 = (f32[1024]{0:T(1024)S(1)}, f32[1024]{0:T(1024)}, u32[]{:S(2)}) copy-start(f32[1024]{0:T(1024)} %param.18) | copy-start | bytes 12292
  78.7 0.7 copy-start.7
  88.4 17.3 %copy-start = (f32[2048,384]{1,0:T(8,128)S(1)}, f32[2048,384]{1,0:T(8,128)}, u32[]{:S(2)}) copy-start(f32[2048,384]{1,0:T(8,128)} %get-tuple-element.17.pre_ref) | copy-start | bytes 9437188
  123.5 72.7 %copy-start.4 = (bf16[256,1024]{1,0:T(8,128)(2,1)S(1)}, bf16[256,1024]{1,0:T(8,128)(2,1)}, u32[]{:S(2)}) copy-start(bf16[256,1024]{1,0:T(8,128)(2,1)} %table_ref.1) | copy-start | bytes 1572868
  123.5 72.7 %copy-start.8 = (f32[256,1024]{1,0:T(8,128)S(1)}, f32[256,1024]{1,0:T(8,128)}, u32[]{:S(2)}) copy-start(f32[256,1024]{1,0:T(8,128)} %param.11) | copy-start | bytes 3145732
  123.5 72.7 %copy-start.9 = (f32[256,1024]{1,0:T(8,128)S(1)}, f32[256,1024]{1,0:T(8,128)}, u32[]{:S(2)}) copy-start(f32[256,1024]{1,0:T(8,128)} %param.12) | copy-start | bytes 3145732

commit v4 on v3

--- a/solution.py
+++ b/solution.py
@@ -98,14 +98,13 @@
         out_ref[pl.ds(q0, FWD_Q), :] = merge_heads(acc).astype(BF)
 
 
-def attend_back_kernel(len_ref, qkv_ref, pre_ref, do_ref, out_ref, dq_ref):
+def attend_back_kernel(len_ref, qkv_ref, do_ref, out_ref, dq_ref):
     tokens = qkv_ref.shape[0]
     ends = ends_of(len_ref)
     dq_ref[...] = jnp.zeros_like(dq_ref)
 
     def finish_part(rows, part, d_part):
-        slope = silu_pair(pre_ref[rows, part * PAIR : (part + 1) * PAIR])[1]
-        out_ref[rows, part * PAIR : (part + 1) * PAIR] = (d_part.astype(BF).astype(F32) * slope).astype(BF)
+        out_ref[rows, part * PAIR : (part + 1) * PAIR] = d_part.astype(BF)
 
     @pl.loop(0, tokens // BACK_K)
     def _(kb):
@@ -163,7 +162,7 @@
     lines = groups // depth
     me = lax.axis_index("group")
     y, z = lax.div(me, depth), lax.rem(me, depth)
-    dy, dz = lax.div(k, depth), lax.rem(k * 3, depth)
+    dy, dz = lax.div(k, depth), lax.rem(k * 5, depth)
     to = lax.rem(y + dy, lines) * depth + lax.rem(z + dz, depth)
     return to
 
@@ -209,16 +208,16 @@
 
 def fetch_kernel(
     groups, seq, names_ref, table_ref, w_ref,
-    emb_ref, pre_ref, qkv_ref, wanted_ref, place_ref, w_all,
-    w_own, table, load_s, w_s, w_r, ask_out, ask_in, row_out, row_in, ring, ask_s, ask_r, row_s, row_r, ring_s, ring_r,
+    emb_ref, slope_ref, pre_u_ref, qkv_ref, wanted_ref, place_ref, w_all,
+    w_vm, table, qkv_out, qkv_in, load_s, keep_s, w_s, w_r,
+    ask_out, ask_in, row_out, row_in, ask_s, ask_r, row_s, row_r, qkv_s, qkv_r,
 ):
     chunks, slots, cut = row_out.shape
     rows = names_ref.shape[1]
     cap = slots // groups
     table_rows, width = table_ref.shape
     wide = 3 * PAIR
-    parts = w_s.shape[0]
-    deep = width // parts
+    half = width // 2
     g, s = lax.axis_index("group"), lax.axis_index("seq")
     chips = seq // 2
     x, core = lax.div(s, 2), lax.rem(s, 2)
@@ -227,26 +226,61 @@
     left = lax.rem(x + chips - 1, chips) * 2 + core
     across = lax.rem(x + 2, chips) * 2 + core
     sib = s + flip
-
-    load_w = pltpu.make_async_copy(w_ref, w_own, load_s.at[0])
+    order = [4, 3, 5, 2, 6, 1, 7]
+
+    load_w = pltpu.make_async_copy(w_ref, w_vm.at[s], load_s.at[0])
     load_table = pltpu.make_async_copy(table_ref, table, load_s.at[1])
     load_w.start()
     load_table.start()
-    barrier, greeted = greet(groups, [sib, right, left], seq)
+    barrier, greeted = greet(groups, [seq_peer(k, seq) for k in range(1, seq)], seq)
     place_ref[...] = slot_places(names_ref[0:1], slots, groups)
     index = jnp.broadcast_to((names_ref[1:2] + 1).astype(F32), (PAIR, rows)).astype(BF)
     ask_out[...] = mm(place_ref[...], index, NT).astype(BF)
     load_w.wait()
-    for j in range(parts):
-        w_own[j * deep : (j + 1) * deep] = by_parts(w_own[j * deep : (j + 1) * deep])
-    keep_w = pltpu.make_async_copy(w_own, w_all.at[pl.ds(pl.multiple_of(s * width, width), width)], load_s.at[2])
-    keep_w.start()
+    for low in (0, half):
+        w_vm[s, low : low + half] = by_parts(w_vm[s, low : low + half])
     pl.semaphore_wait(barrier, greeted)
 
-    def w_hop(j, op, block, to, low=0, size=deep):
-        at = pl.ds(pl.multiple_of(block * width + j * deep + low, size), size)
-        src = w_own.at[pl.ds(j * deep, deep)] if op < 3 else w_all.at[at]
-        return send(src, w_all.at[at], w_s.at[j, op], w_r.at[j, op], seq=to)
+    def w_hop(j, op, block, to, low=0, size=width):
+        view = w_vm.at[block, pl.ds(low, size), (wide if j else 0) : (4 * PAIR if j else wide)]
+        return send(view, view, w_s.at[j, op], w_r.at[j, op], seq=to)
+
+    def w_start(j):
+        w_hop(j, 1, s, right).start()
+        w_hop(j, 2, s, left).start()
+        w_hop(j, 0, s, sib).start()
+
+    def w_first(j):
+        w_hop(j, 1, left, right).wait_recv()
+        w_hop(j, 3, left, right, 0, half).start()
+        w_hop(j, 4, left, sib).start()
+        w_hop(j, 2, right, left).wait_recv()
+        w_hop(j, 5, right, left, half, half).start()
+        w_hop(j, 6, right, sib).start()
+
+    def w_second(j):
+        w_hop(j, 3, across, right, 0, half).wait_recv()
+        w_hop(j, 7, across, sib, 0, half).start()
+        w_hop(j, 5, across, left, half, half).wait_recv()
+        w_hop(j, 8, across, sib, half, half).start()
+
+    def w_last(j):
+        w_hop(j, 0, sib, sib).wait_recv()
+        w_hop(j, 4, left + flip, sib).wait_recv()
+        w_hop(j, 6, right + flip, sib).wait_recv()
+        w_hop(j, 7, across + flip, sib, 0, half).wait_recv()
+        w_hop(j, 8, across + flip, sib, half, half).wait_recv()
+
+    def w_sent(j):
+        w_hop(j, 0, s, sib).wait_send()
+        w_hop(j, 1, s, right).wait_send()
+        w_hop(j, 2, s, left).wait_send()
+        w_hop(j, 3, left, right, 0, half).wait_send()
+        w_hop(j, 4, left, sib).wait_send()
+        w_hop(j, 5, right, left, half, half).wait_send()
+        w_hop(j, 6, right, sib).wait_send()
+        w_hop(j, 7, across, sib, 0, half).wait_send()
+        w_hop(j, 8, across, sib, half, half).wait_send()
 
     mine = pl.ds(pl.multiple_of(g * cap, cap), cap)
 
@@ -267,10 +301,7 @@
     def _(k):
         ask(k).start()
 
-    for j in range(parts):
-        w_hop(j, 1, s, right).start()
-        w_hop(j, 2, s, left).start()
-        w_hop(j, 0, s, sib).start()
+    w_start(0)
     ask_in[mine] = ask_out[mine]
 
     @pl.loop(1, groups)
@@ -288,139 +319,66 @@
 
         @pl.loop(1, groups)
         def _(k):
-            if c > 0:
-                give(c - 1, k).wait_send()
             give(c, k).start()
 
         row_in[c, mine] = row_out[c, mine]
-
-    half = rows // 2
-
-    def hop(c, op, block, to, low=0, size=rows):
-        view = ring.at[c, block, pl.ds(low, size)]
-        return send(view, view, ring_s.at[c, op], ring_r.at[c, op], seq=to)
-
-    def project(c, block):
-        at = pl.ds(pl.multiple_of(block * rows, rows), rows)
-        val = mm(ring[c, block], w_own[c * cut : (c + 1) * cut, :wide])
-        if c > 0:
-            val = val + pre_ref[at]
-        pre_ref[at] = val
-        if c == chunks - 1:
-            qkv_ref[at] = silu_pair(val)[0].astype(BF)
 
     def gathered(c):
         @pl.loop(1, groups)
         def _(k):
-            give(c, k).wait_recv()
-            if c == chunks - 1:
-                give(c, k).wait_send()
-
-        block = mm(place_ref[...], row_in[c], TN).astype(BF)
-        emb_ref[:, c * cut : (c + 1) * cut] = block
-        ring[c, s] = block
-        hop(c, 1, s, right).start()
-        hop(c, 2, s, left).start()
-        hop(c, 0, s, sib).start()
-        project(c, s)
-
-    def first_hop(c):
-        hop(c, 1, left, right).wait_recv()
-        hop(c, 3, left, right, 0, half).start()
-        hop(c, 4, left, sib).start()
-        hop(c, 2, right, left).wait_recv()
-        hop(c, 5, right, left, half, half).start()
-        hop(c, 6, right, sib).start()
-        project(c, left)
-        project(c, right)
-        hop(c, 0, sib, sib).wait_recv()
-        project(c, sib)
-
-    def second_hop(c):
-        hop(c, 3, across, right, 0, half).wait_recv()
-        hop(c, 7, across, sib, 0, half).start()
-        hop(c, 5, across, left, half, half).wait_recv()
-        hop(c, 8, across, sib, half, half).start()
-        project(c, across)
-
-    def from_sibling(c):
-        hop(c, 4, left + flip, sib).wait_recv()
-        project(c, left + flip)
-        hop(c, 6, right + flip, sib).wait_recv()
-        project(c, right + flip)
-        hop(c, 7, across + flip, sib, 0, half).wait_recv()
-        hop(c, 8, across + flip, sib, half, half).wait_recv()
-        project(c, across + flip)
-
+            give(c, k).wait()
+
+        emb_ref[:, c * cut : (c + 1) * cut] = mm(place_ref[...], row_in[c], TN).astype(BF)
+
+    w_first(0)
+    w_start(1)
+    w_second(0)
     for c in range(chunks):
         gathered(c)
-        if c == 0:
-            for j in range(parts):
-                w_hop(j, 1, left, right).wait_recv()
-                w_hop(j, 3, left, right, 0, deep // 2).start()
-                w_hop(j, 4, left, sib).start()
-                w_hop(j, 2, right, left).wait_recv()
-                w_hop(j, 5, right, left, deep // 2, deep // 2).start()
-                w_hop(j, 6, right, sib).start()
-        if c > 0:
-            second_hop(c - 1)
-        first_hop(c)
-        if c > 0:
-            from_sibling(c - 1)
-    second_hop(chunks - 1)
-    from_sibling(chunks - 1)
-
-    for j in range(parts):
-        w_hop(j, 3, across, right, 0, deep // 2).wait_recv()
-        w_hop(j, 7, across, sib, 0, deep // 2).start()
-        w_hop(j, 5, across, left, deep // 2, deep // 2).wait_recv()
-        w_hop(j, 8, across, sib, deep // 2, deep // 2).start()
-    for j in range(parts):
-        w_hop(j, 0, sib, sib).wait_recv()
-        w_hop(j, 4, left + flip, sib).wait_recv()
-        w_hop(j, 6, right + flip, sib).wait_recv()
-        w_hop(j, 7, across + flip, sib, 0, deep // 2).wait_recv()
-        w_hop(j, 8, across + flip, sib, deep // 2, deep // 2).wait_recv()
-        w_hop(j, 0, s, sib).wait_send()
-        w_hop(j, 1, s, right).wait_send()
-        w_hop(j, 2, s, left).wait_send()
-        w_hop(j, 3, left, right, 0, deep // 2).wait_send()
-        w_hop(j, 4, left, sib).wait_send()
-        w_hop(j, 5, right, left, deep // 2, deep // 2).wait_send()
-        w_hop(j, 6, right, sib).wait_send()
-        w_hop(j, 7, across, sib, 0, deep // 2).wait_send()
-        w_hop(j, 8, across, sib, deep // 2, deep // 2).wait_send()
-    keep_w.wait()
-    for c in range(chunks):
-        hop(c, 1, s, right).wait_send()
-        hop(c, 2, s, left).wait_send()
-        hop(c, 0, s, sib).wait_send()
-        hop(c, 3, left, right, 0, half).wait_send()
-        hop(c, 4, left, sib).wait_send()
-        hop(c, 5, right, left, half, half).wait_send()
-        hop(c, 6, right, sib).wait_send()
-        hop(c, 7, across, sib, 0, half).wait_send()
-        hop(c, 8, across, sib, half, half).wait_send()
+    w_last(0)
+    w_first(1)
+
+    def share(k):
+        to = seq_peer(k, seq)
+        return send(qkv_out.at[to], qkv_in.at[s], qkv_s.at[k], qkv_r.at[k], seq=to)
+
+    def keep(b):
+        return pltpu.make_async_copy(w_vm.at[b], w_all.at[pl.ds(b * width, width)], keep_s.at[b])
+
+    for k in order + [0]:
+        to = seq_peer(k, seq)
+        act, slope = silu_pair(mm(emb_ref[...], w_vm[to, :, :wide]))
+        qkv_out[to] = act.astype(BF)
+        slope_ref[to] = slope
+        if k > 0:
+            share(k).start()
+    qkv_in[s] = qkv_out[s]
+    w_second(1)
+    w_last(1)
+    for b in range(seq):
+        pre_u_ref[b] = mm(emb_ref[...], w_vm[b, :, wide:])
+        keep(b).start()
+    w_sent(0)
+    w_sent(1)
+    for b in range(seq):
+        keep(b).wait()
+    for k in order:
+        share(k).wait()
+    for b in range(seq):
+        qkv_ref[b * rows : (b + 1) * rows] = qkv_in[b]
 
 
 def middle_kernel(
-    seq, att_ref, emb_ref, w_ref, wo_ref, gain_ref, up_ref,
+    seq, att_ref, emb_ref, pre_u_ref, wo_ref, gain_ref, up_ref,
     layer_ref, dheads_ref, dpu_ref,
-    wu, wo, mixed, att_in, datt_out, datt_in, d_mixed, pre_u, w_s, wo_s, att_s, att_r, datt_s, datt_r,
+    wo, mixed, att_in, datt_out, datt_in, d_mixed, wo_s, att_s, att_r, datt_s, datt_r,
 ):
     rows, width = emb_ref.shape
     s = lax.axis_index("seq")
     order = [4, 3, 5, 2, 6, 1, 7]
 
-    def load(b):
-        return pltpu.make_async_copy(
-            w_ref.at[pl.ds(b * width, width), 3 * PAIR : 4 * PAIR], wu.at[b], w_s.at[b]
-        )
-
     load_wo = pltpu.make_async_copy(wo_ref, wo, wo_s)
     load_wo.start()
-    for b in range(seq):
-        load(b).start()
     barrier, greeted = greet(1, [seq_peer(k, seq) for k in range(1, seq)], seq)
     pl.semaphore_wait(barrier, greeted)
 
@@ -445,9 +403,6 @@
     load_wo.wait()
     d_mixed[...] = mm(up_ref[...], wo[...], NT)
     emb = emb_ref[...]
-    for b in range(seq):
-        load(b).wait()
-        pre_u[:, b * PAIR : (b + 1) * PAIR] = mm(emb, wu[b])
     gain = gain_ref[...]
     for h in range(HALVES):
         part = slice(h * half, (h + 1) * half)
@@ -458,7 +413,7 @@
         spread = jnp.mean(center * center, axis=-1, keepdims=True)
         r = lax.rsqrt(spread + norm_eps)
         xhat = center * r
-        act_u, slope_u = silu_pair(pre_u[part])
+        act_u, slope_u = silu_pair(jnp.concatenate([pre_u_ref[b, part] for b in range(seq)], axis=1))
         u = act_u.astype(BF).astype(F32)
         d_mix = d_mixed[part]
         gx = d_mix * u * gain
@@ -487,9 +442,9 @@
 
 
 def back_kernel(
-    groups, seq, dqkv_ref, dpu_ref, place_ref, wanted_ref, w_ref, up_ref,
+    groups, seq, dqkv_ref, dpu_ref, place_ref, wanted_ref, w_ref, slope_ref, up_ref,
     grad_ref,
-    w_vm, d_in, row_out, row_in, part, part_f, part_in, share, share_in,
+    w_vm, slope, slope_s, d_in, row_out, row_in, part, part_f, part_in, share, share_in,
     w_s, d_s, d_r, row_s, row_r, part_s, part_r, share_s, share_r,
 ):
     chunks, slots, cut = row_out.shape
@@ -503,6 +458,8 @@
     def load(b):
         return pltpu.make_async_copy(w_ref.at[pl.ds(b * width, width)], w_vm.at[b], w_s.at[b])
 
+    load_slope = pltpu.make_async_copy(slope_ref, slope, slope_s)
+    load_slope.start()
     for b in range(seq):
         load(b).start()
     barrier, greeted = greet(groups, [seq_peer(k, seq) for k in range(1, seq)], seq)
@@ -546,6 +503,7 @@
 
     for k in order:
         hand(k).start()
+    load_slope.wait()
     for b in range(seq):
         load(b).wait()
 
@@ -556,6 +514,8 @@
             b = lax.rem(s + seq - k, seq)
             if c == 0 and k > 0:
                 hand(k).wait_recv()
+            if c == 0:
+                d_in[b, :, :wide] = (d_in[b, :, :wide].astype(F32) * slope[b]).astype(BF)
             total = total + mm(d_in[b], w_vm[b, cols, :], NT)
         row_out[c] = mm(place_ref[...], total.astype(BF)).astype(BF)
 
@@ -637,7 +597,6 @@
 ANY = pl.BlockSpec(memory_space=pl.ANY)
 HBM = pl.BlockSpec(memory_space=pltpu.HBM)
 CHUNKS = 2
-W_PARTS = 2
 HALVES = 2
 DMA = pltpu.SemaphoreType.DMA
 
@@ -677,12 +636,13 @@
 
     cut = width // CHUNKS
 
-    embedded, pre, qkv, wanted, place, w_all = remote_call(
+    embedded, slope, pre_u, qkv, wanted, place, w_all = remote_call(
         functools.partial(fetch_kernel, groups, seq),
         1,
         (
             sds((tok_rows, width), BF),
-            sds((tokens, 3 * PAIR), F32),
+            sds((seq, tok_rows, 3 * PAIR), F32),
+            sds((seq, tok_rows, PAIR), F32),
             sds((tokens, 3 * PAIR), BF),
             sds((slots, table_rows), BF),
             sds((slots, tok_rows), BF),
@@ -690,24 +650,26 @@
         ),
         [VM, HBM, HBM],
         [
-            pltpu.VMEM((width, 4 * PAIR), BF),
+            pltpu.VMEM((seq, width, 4 * PAIR), BF),
             pltpu.VMEM((table_rows, width), BF),
-            DMA((3,)),
-            DMA((W_PARTS, 9)),
-            DMA((W_PARTS, 9)),
+            pltpu.VMEM((seq, tok_rows, 3 * PAIR), BF),
+            pltpu.VMEM((seq, tok_rows, 3 * PAIR), BF),
+            DMA((2,)),
+            DMA((seq,)),
+            DMA((2, 9)),
+            DMA((2, 9)),
             pltpu.VMEM((slots, PAIR), BF),
             pltpu.VMEM((slots, PAIR), BF),
             pltpu.VMEM((CHUNKS, slots, cut), BF),
             pltpu.VMEM((CHUNKS, slots, cut), BF),
-            pltpu.VMEM((CHUNKS, seq, tok_rows, cut), BF),
             DMA((groups,)),
             DMA((groups,)),
             DMA((CHUNKS, groups)),
             DMA((CHUNKS, groups)),
-            DMA((CHUNKS, 9)),
-            DMA((CHUNKS, 9)),
+            DMA((seq,)),
+            DMA((seq,)),
         ],
-        (VM,) * 5 + (HBM,),
+        (VM,) * 6 + (HBM,),
     )(jnp.stack([row_owner[:, 0], row_index]), embed_table, proj_weight)
 
     att_heads = local_call(attend_kernel, sds((tokens, PAIR), BF), [SM, VM])(lengths, qkv)
@@ -719,38 +681,37 @@
             sds((seq, tok_rows, PAIR), BF),
             sds((seq, tok_rows, PAIR), BF),
         ),
-        [VM, VM, ANY, ANY, VM, VM],
+        [VM, VM, VM, ANY, VM, VM],
         [
-            pltpu.VMEM((seq, width, PAIR), BF),
             pltpu.VMEM((width, width), BF),
             pltpu.VMEM((tok_rows, width), BF),
             pltpu.VMEM((seq, tok_rows, PAIR), BF),
             pltpu.VMEM((seq, tok_rows, PAIR), BF),
             pltpu.VMEM((seq, tok_rows, PAIR), BF),
             pltpu.VMEM((tok_rows, width), F32),
-            pltpu.VMEM((tok_rows, width), F32),
-            DMA((seq,)),
             DMA,
             DMA((HALVES, seq)),
             DMA((HALVES, seq)),
             DMA((HALVES, seq)),
             DMA((HALVES, seq)),
         ],
-    )(att_heads, embedded, w_all, out_weight, norm_gain.reshape(1, -1), upstream)
-    d_pre_heads = local_call(
+    )(att_heads, embedded, pre_u, out_weight, norm_gain.reshape(1, -1), upstream)
+    d_qkv_heads = local_call(
         attend_back_kernel,
         sds((tokens, 3 * PAIR), BF),
-        [SM, VM, VM, VM],
+        [SM, VM, VM],
         [pltpu.VMEM((tokens, PAIR), F32)],
-    )(lengths, qkv, pre, d_heads.reshape(tokens, PAIR))
+    )(lengths, qkv, d_heads.reshape(tokens, PAIR))
     own = table_rows // seq
     row_grad = remote_call(
         functools.partial(back_kernel, groups, seq),
         3,
         sds((table_rows, width), F32),
-        [VM, VM, VM, VM, ANY, VM],
+        [VM, VM, VM, VM, ANY, ANY, VM],
         [
             pltpu.VMEM((seq, width, 4 * PAIR), BF),
+            pltpu.VMEM((seq, tok_rows, 3 * PAIR), F32),
+            DMA,
             pltpu.VMEM((seq, tok_rows, 4 * PAIR), BF),
             pltpu.VMEM((CHUNKS, slots, cut), BF),
             pltpu.VMEM((CHUNKS, slots, cut), BF),
@@ -769,7 +730,7 @@
             DMA((CHUNKS, seq)),
             DMA((CHUNKS, seq)),
         ],
-    )(d_pre_heads, d_pre_u, place, wanted, w_all, upstream)
+    )(d_qkv_heads, d_pre_u, place, wanted, w_all, slope, upstream)
     new_table, new_moment, new_second = adam_update(embed_table, adam_m, adam_v, row_grad)
     return (layer_out, new_table, new_moment, new_second)
 

time: 200 us -> 192 us (0.960)
  Pallas kernels: 192 us -> 184 us
    pallas_call x1, Pallas kernels: 75 us -> 70.7 us  [body(): remote_call(functools.partial(fetch_kernel, groups, seq), 1, (sds((tok_ro...]
    pallas_call x1, Pallas kernels: 17.8 us -> 15.4 us  [body(): local_call(attend_back_kernel, sds((tokens, 3 * PAIR), BF), [SM, VM, VM],...]
where the time goes in v4:
time: 192 us
  Pallas kernels  184 us (96%)
  local copies, waits for them, and re-layouts  3.91 us (2%)
  other arithmetic  3.04 us (2%)
    pallas_call x1, Pallas kernels, body(): remote_call(functools.partial(back_kernel, groups, seq), 3, sds((table_ro...  72.5 us
    pallas_call x1, Pallas kernels, body(): remote_call(functools.partial(fetch_kernel, groups, seq), 1, (sds((tok_ro...  70.7 us
    pallas_call x1, Pallas kernels, body(): remote_call(functools.partial(middle_kernel, seq), 2, (sds((tok_rows, wid...  16.9 us
    pallas_call x1, Pallas kernels, body(): local_call(attend_back_kernel, sds((tokens, 3 * PAIR), BF), [SM, VM, VM],...  15.4 us
    pallas_call x1, Pallas kernels, body(): local_call(attend_kernel, sds((tokens, PAIR), BF), [SM, VM])(lengths, qkv)  8.34 us
    unnamed x17, local copies, waits for them, and re-layouts  3.91 us

profile of v4, /device:TPU:1, one launch (start us, length us, event | category | flops | bytes accessed | tf_op | source)
XLA Modules:
  0.0 191.5 jit_solution(7331744437176099236)
XLA Ops:
  0.6 0.0 copy-start
  0.6 0.8 pad_add_fusion.names_ref
  1.4 0.0 copy-start.1
  1.4 1.0 copy-done.1
  2.4 0.0 copy-start.3
  2.4 1.2 copy-done.3
  3.7 0.0 copy-start.4
  3.7 70.7 %shard_map.129 = (bf16[256,1024]{1,0:T(8,128)(2,1)S(1)}, f32[8,256,384]{2,1,0:T(8,128)}, f32[8,256,128]{2,1,0:T(8,128)S(1)}, bf16[2048,384]{1,0:T(8,128)(2,1)S(1...) custom-call(s32[2,256]{1,0:T(2,128)S(1)} %pad_add_fusion.names_ref, ...), custom_call_target="tpu_custom_call" | custom-call | tf_op jit(solution)/shard_map/pallas_call | solution.py:639
  74.4 0.0 copy-start.5
  74.4 0.6 copy-done.5
  75.0 8.3 %shard_map.130.att_ref = bf16[2048,128]{1,0:T(8,128)(2,1)S(1)} custom-call(s32[1,4]{1,0:T(1,128)S(1)} %copy-done.5, bf16[2048,384]{1,0:T(8,128)(2,1)S(1)} %get-tuple-element.14.qkv_ref), custom_call_target="tpu_custom_call" | custom-call | tf_op jit(solution)/shard_map/pallas_call | solution.py:675
  83.4 0.0 copy-done
  83.4 0.0 copy-done.4
  83.4 16.9 %shard_map.131 = (f32[256,1024]{1,0:T(8,128)S(1)}, bf16[8,256,128]{2,1,0:T(8,128)(2,1)S(1)}, bf16[8,256,128]{2,1,0:T(8,128)(2,1)S(1)}) custom-call(bf16[2048,128]{1,0:T(8,128)(2,1)S(1)} %shard_map.130.att_ref, bf16[256,1024]{1,0:T(8,128)(2,1)S(1)} %get-tuple-element.15.emb_ref, f32[8,256,128]{2,1,0:T(8,128)S(1)} %get-tuple-element.16.pre_u_ref, ...), custom_call_target="tpu_custom_call" | custom-call | tf_op jit(solution)/shard_map/pallas_call | solution.py:676
  100.3 15.4 %shard_map.132.dqkv_ref = bf16[2048,384]{1,0:T(8,128)(2,1)S(1)} custom-call(s32[1,4]{1,0:T(1,128)S(1)} %copy-done.5, bf16[2048,384]{1,0:T(8,128)(2,1)S(1)} %get-tuple-element.14.qkv_ref, bf16[2048,128]{1,0:T(8,128)(2,1)S(1)} %bitcast.4), custom_call_target="tpu_custom_call" | custom-call | tf_op jit(solution)/shard_map/pallas_call | solution.py:699
  115.7 0.0 copy-start.2
  115.8 0.0 copy-start.6
  115.8 0.0 copy-start.7
  115.8 72.5 %shard_map.133 = f32[256,1024]{1,0:T(8,128)S(1)} custom-call(bf16[2048,384]{1,0:T(8,128)(2,1)S(1)} %shard_map.132.dqkv_ref, bf16[8,256,128]{2,1,0:T(8,128)(2,1)S(1)} %get-tuple-element.19.dpu_ref, bf16[512,256]{1,0:T(8,128)(2,1)S(1)} %get-tuple-element.20.place_ref, bf16[512,256]{1,0:T(8,128)(2,1)S(1)} %get-tuple-element.21.wanted_ref, ...), custom_call_target="tpu_custom_call" | custom-call | tf_op jit(solution)/shard_map/pallas_call | solution.py:706
  188.3 0.0 copy-done.2
  188.3 0.0 copy-done.6
  188.3 0.0 copy-done.7
  188.3 2.3 %multiply_subtract_fusion = (f32[256,1024]{1,0:T(8,128)}, f32[256,1024]{1,0:T(8,128)}, f32[256,1024]{1,0:T(8,128)}) fusion(bf16[256,1024]{1,0:T(8,128)(2,1)S(1)} %copy-done.2, f32[256,1024]{1,0:T(8,128)S(1)} %shard_map.133, f32[256,1024]{1,0:T(8,128)S(1)} %copy-done.6, f32[256,1024]{1,0:T(8,128)S(1)} %copy-done.7), kind=kLoop, calls=%fused_computation.2 | loop fusion | flops 3670016 | bytes 6815744 | tf_op jit(solution)/shard_map/sub | solution.py:612
  190.6 1.0 copy.15
Async XLA Ops:
  0.6 82.7 %copy-start = (bf16[256,1024]{1,0:T(8,128)(2,1)S(1)}, bf16[256,1024]{1,0:T(8,128)(2,1)}, u32[]{:S(2)}) copy-start(bf16[256,1024]{1,0:T(8,128)(2,1)} %up_ref.3) | copy-start | bytes 1572868
  1.4 1.0 copy-start.1
  2.4 1.2 copy-start.3
  3.7 79.7 %copy-start.4 = (f32[1024]{0:T(1024)S(1)}, f32[1024]{0:T(1024)}, u32[]{:S(2)}) copy-start(f32[1024]{0:T(1024)} %param.18) | copy-start | bytes 12292
  74.4 0.7 copy-start.5
  115.7 72.5 %copy-start.2 = (bf16[256,1024]{1,0:T(8,128)(2,1)S(1)}, bf16[256,1024]{1,0:T(8,128)(2,1)}, u32[]{:S(2)}) copy-start(bf16[256,1024]{1,0:T(8,128)(2,1)} %table_ref.1) | copy-start | bytes 1572868
  115.8 72.5 %copy-start.6 = (f32[256,1024]{1,0:T(8,128)S(1)}, f32[256,1024]{1,0:T(8,128)}, u32[]{:S(2)}) copy-start(f32[256,1024]{1,0:T(8,128)} %param.11) | copy-start | bytes 3145732
  115.8 72.5 %copy-start.7 = (f32[256,1024]{1,0:T(8,128)S(1)}, f32[256,1024]{1,0:T(8,128)}, u32[]{:S(2)}) copy-start(f32[256,1024]{1,0:T(8,128)} %param.12) | copy-start | bytes 3145732

commit v5 on v4

--- a/solution.py
+++ b/solution.py
@@ -670,6 +670,7 @@
             DMA((seq,)),
         ],
         (VM,) * 6 + (HBM,),
+        limit=57,
     )(jnp.stack([row_owner[:, 0], row_index]), embed_table, proj_weight)
 
     att_heads = local_call(attend_kernel, sds((tokens, PAIR), BF), [SM, VM])(lengths, qkv)

time: 192 us -> 193 us (level)
  Pallas kernels: 184 us -> 186 us
    pallas_call x1, Pallas kernels: 72.5 us -> 63.7 us  [body(): remote_call(functools.partial(back_kernel, groups, seq), 3, sds((table_ro...]
    pallas_call x1, Pallas kernels: 15.4 us -> 21.7 us  [body(): local_call(attend_back_kernel, sds((tokens, 3 * PAIR), BF), [SM, VM, VM],...]
    pallas_call x1, Pallas kernels: 8.34 us -> 11.2 us  [body(): local_call(attend_kernel, sds((tokens, PAIR), BF), [SM, VM])(lengths, qkv)]
    unnamed x17 -> x27, local copies, waits for them, and re-layouts: 3.91 us -> 3.08 us
where the time goes in v5:
time: 193 us
  Pallas kernels  186 us (96%)
  other arithmetic  3.53 us (2%)
  local copies, waits for them, and re-layouts  3.08 us (2%)
    pallas_call x1, Pallas kernels, body(): remote_call(functools.partial(fetch_kernel, groups, seq), 1, (sds((tok_ro...  72 us
    pallas_call x1, Pallas kernels, body(): remote_call(functools.partial(back_kernel, groups, seq), 3, sds((table_ro...  63.7 us
    pallas_call x1, Pallas kernels, body(): local_call(attend_back_kernel, sds((tokens, 3 * PAIR), BF), [SM, VM, VM],...  21.7 us
    pallas_call x1, Pallas kernels, body(): remote_call(functools.partial(middle_kernel, seq), 2, (sds((tok_rows, wid...  16.9 us
    pallas_call x1, Pallas kernels, body(): local_call(attend_kernel, sds((tokens, PAIR), BF), [SM, VM])(lengths, qkv)  11.2 us

profile of v5, /device:TPU:1, one launch (start us, length us, event | category | flops | bytes accessed | tf_op | source)
XLA Modules:
  0.0 193.1 jit_solution(818269347166349808)
XLA Ops:
  0.6 0.0 copy-start.2
  0.6 0.0 copy-start.7
  0.7 1.3 pad_add_fusion.names_ref
  2.0 72.0 %shard_map.129 = (bf16[256,1024]{1,0:T(8,128)(2,1)}, f32[8,256,384]{2,1,0:T(8,128)}, f32[8,256,128]{2,1,0:T(8,128)}, bf16[2048,384]{1,0:T(8,128)(2,1)}, bf16[512...) custom-call(s32[2,256]{1,0:T(2,128)} %pad_add_fusion.names_ref, ...), custom_call_target="tpu_custom_call" | custom-call | tf_op jit(solution)/shard_map/pallas_call | solution.py:639
  74.0 0.0 copy-start
  74.0 1.4 copy-done
  75.4 0.0 copy-start.8
  75.4 0.7 copy-done.8
  76.1 0.0 copy-start.3
  76.1 0.0 copy-start.4
  76.1 11.2 %shard_map.130.att_ref = bf16[2048,128]{1,0:T(8,128)(2,1)S(1)} custom-call(s32[1,4]{1,0:T(1,128)S(1)} %copy-done.8, bf16[2048,384]{1,0:T(8,128)(2,1)S(1)} %copy-done), custom_call_target="tpu_custom_call" | custom-call | tf_op jit(solution)/shard_map/pallas_call | solution.py:676
  87.3 0.0 copy-done.2
  87.3 0.0 copy-done.7
  87.3 0.0 copy-done.3
  87.3 0.0 copy-done.4
  87.3 0.0 copy-start.1
  87.3 0.0 copy-start.9
  87.4 16.9 %shard_map.131 = (f32[256,1024]{1,0:T(8,128)S(1)}, bf16[8,256,128]{2,1,0:T(8,128)(2,1)S(1)}, bf16[8,256,128]{2,1,0:T(8,128)(2,1)S(1)}) custom-call(bf16[2048,128]{1,0:T(8,128)(2,1)S(1)} %shard_map.130.att_ref, bf16[256,1024]{1,0:T(8,128)(2,1)S(1)} %copy-done.4, f32[8,256,128]{2,1,0:T(8,128)S(1)} %copy-done.3, bf16[1024,1024]{1,0:T(8,128)(2,1)} %wo_ref.1, ...), custom_call_target="tpu_custom_call" | custom-call | tf_op jit(solution)/shard_map/pallas_call | solution.py:677
  104.3 0.0 copy-start.5
  104.3 0.0 copy-start.6
  104.3 0.0 copy-done.1
  104.3 0.0 copy-done.9
  104.3 21.7 %shard_map.132.dqkv_ref = bf16[2048,384]{1,0:T(8,128)(2,1)S(1)} custom-call(s32[1,4]{1,0:T(1,128)S(1)} %copy-done.9, bf16[2048,384]{1,0:T(8,128)(2,1)S(1)} %copy-done.1, bf16[2048,128]{1,0:T(8,128)(2,1)S(1)} %bitcast.4), custom_call_target="tpu_custom_call" | custom-call | tf_op jit(solution)/shard_map/pallas_call | solution.py:700
  126.1 0.0 copy-done.5
  126.1 0.0 copy-done.6
  126.1 0.0 copy-start.10
  126.1 0.0 copy-start.11
  126.1 0.0 copy-start.12
  126.1 63.7 %shard_map.133 = f32[256,1024]{1,0:T(8,128)S(1)} custom-call(bf16[2048,384]{1,0:T(8,128)(2,1)S(1)} %shard_map.132.dqkv_ref, bf16[8,256,128]{2,1,0:T(8,128)(2,1)S(1)} %get-tuple-element.19.dpu_ref, bf16[512,256]{1,0:T(8,128)(2,1)S(1)} %copy-done.6, bf16[512,256]{1,0:T(8,128)(2,1)S(1)} %copy-done.5, bf16[8192,512]{1,0:T(8,128)(2,1)} %get-tuple-element.22.w_ref, ...), custom_call_target="tpu_custom_call" | custom-call | tf_op jit(solution)/shard_map/pallas_call | solution.py:707
  189.9 0.0 copy-done.10
  189.9 0.0 copy-done.11
  189.9 0.0 copy-done.12
  189.9 2.2 %multiply_subtract_fusion = (f32[256,1024]{1,0:T(8,128)}, f32[256,1024]{1,0:T(8,128)}, f32[256,1024]{1,0:T(8,128)}) fusion(bf16[256,1024]{1,0:T(8,128)(2,1)S(1)} %copy-done.10, f32[256,1024]{1,0:T(8,128)S(1)} %shard_map.133, f32[256,1024]{1,0:T(8,128)S(1)} %copy-done.11, f32[256,1024]{1,0:T(8,128)S(1)} %copy-done.12), kind=kLoop, calls=%fused_computation.2 | loop fusion | flops 3670016 | bytes 6815744 | tf_op jit(solution)/shard_map/sub | solution.py:612
  192.1 1.0 copy.15
Async XLA Ops:
  0.6 86.7 %copy-start.2 = (bf16[256,1024]{1,0:T(8,128)(2,1)S(1)}, bf16[256,1024]{1,0:T(8,128)(2,1)}, u32[]{:S(2)}) copy-start(bf16[256,1024]{1,0:T(8,128)(2,1)} %up_ref.3) | copy-start | bytes 1572868
  0.6 86.7 %copy-start.7 = (f32[1024]{0:T(1024)S(1)}, f32[1024]{0:T(1024)}, u32[]{:S(2)}) copy-start(f32[1024]{0:T(1024)} %param.18) | copy-start | bytes 12292
  74.0 1.4 copy-start
  75.4 0.7 copy-start.8
  76.1 11.3 %copy-start.3 = (f32[8,256,128]{2,1,0:T(8,128)S(1)}, f32[8,256,128]{2,1,0:T(8,128)}, u32[]{:S(2)}) copy-start(f32[8,256,128]{2,1,0:T(8,128)} %get-tuple-element.16.pre_u_ref) | copy-start | bytes 3145732
  76.1 11.3 %copy-start.4 = (bf16[256,1024]{1,0:T(8,128)(2,1)S(1)}, bf16[256,1024]{1,0:T(8,128)(2,1)}, u32[]{:S(2)}) copy-start(bf16[256,1024]{1,0:T(8,128)(2,1)} %get-tuple-element.15.emb_ref) | copy-start | bytes 1572868
  87.3 17.0 %copy-start.1 = (bf16[2048,384]{1,0:T(8,128)(2,1)S(1)}, bf16[2048,384]{1,0:T(8,128)(2,1)}, u32[]{:S(2)}) copy-start(bf16[2048,384]{1,0:T(8,128)(2,1)} %get-tuple-element.14.qkv_ref) | copy-start | bytes 4718596
  87.3 17.0 %copy-start.9 = (s32[1,4]{1,0:T(1,128)S(1)}, s32[1,4]{1,0:T(1,128)}, u32[]{:S(2)}) copy-start(s32[1,4]{1,0:T(1,128)} %len_ref.3) | copy-start | bytes 52
  104.3 21.8 %copy-start.5 = (bf16[512,256]{1,0:T(8,128)(2,1)S(1)}, bf16[512,256]{1,0:T(8,128)(2,1)}, u32[]{:S(2)}) copy-start(bf16[512,256]{1,0:T(8,128)(2,1)} %get-tuple-element.21.wanted_ref) | copy-start | bytes 786436
  104.3 21.8 %copy-start.6 = (bf16[512,256]{1,0:T(8,128)(2,1)S(1)}, bf16[512,256]{1,0:T(8,128)(2,1)}, u32[]{:S(2)}) copy-start(bf16[512,256]{1,0:T(8,128)(2,1)} %get-tuple-element.20.place_ref) | copy-start | bytes 786436
  126.1 63.8 %copy-start.10 = (bf16[256,1024]{1,0:T(8,128)(2,1)S(1)}, bf16[256,1024]{1,0:T(8,128)(2,1)}, u32[]{:S(2)}) copy-start(bf16[256,1024]{1,0:T(8,128)(2,1)} %table_ref.1) | copy-start | bytes 1572868
  126.1 63.8 %copy-start.11 = (f32[256,1024]{1,0:T(8,128)S(1)}, f32[256,1024]{1,0:T(8,128)}, u32[]{:S(2)}) copy-start(f32[256,1024]{1,0:T(8,128)} %param.11) | copy-start | bytes 3145732
  126.1 63.8 %copy-start.12 = (f32[256,1024]{1,0:T(8,128)S(1)}, f32[256,1024]{1,0:T(8,128)}, u32[]{:S(2)}) copy-start(f32[256,1024]{1,0:T(8,128)} %param.12) | copy-start | bytes 3145732
